TPU v7x, 32 devices: a whole 2x2x4 slice. The times are simulated.
32 devices in a mesh: expert: 4 (over y, core), context: 2 (over x), dp: 4 (over z).
Axes of the slice: x: 2, y: 2, z: 4, core: 2. Of those that a mesh axis runs over, the one named last changes fastest.
Arguments:
- tokens: bfloat16 [8, 8, 1024, 512], P('dp', 'expert', 'context'), may hold values from -6 to 6
- gain_attn: float32 [512], replicated, may hold values from 0.5 to 1.5
- query_key_value_weight: bfloat16 [512, 1536], replicated, may hold values from -0.25 to 0.25
- w_out: bfloat16 [512, 512], replicated, may hold values from -2 to 2
- gain_mix: float32 [512], replicated, may hold values from 0.5 to 1.5
- w_control: bfloat16 [512, 8], replicated, may hold values from -0.25 to 0.25
- w_in: bfloat16 [8, 512, 2048], P('expert'), may hold values from -1.5 to 1.5
- w_back: bfloat16 [8, 2048, 512], P('expert'), may hold values from -1 to 1
- segments: int32 [8, 8, 1024], P('dp', 'expert'), may hold values from 0 to 2, as said below
- valid: int32 [8, 8, 1024], P('dp', 'expert'), may hold values from 0 to 1, as said below
- cotangent: bfloat16 [8, 8, 1024, 512], P('dp', 'expert', 'context'), may hold values from -6 to 6
Outputs:
- output: bfloat16 [8, 8, 1024, 512], P('dp', 'expert', 'context')
- d_tokens: bfloat16 [8, 8, 1024, 512], P('dp', 'expert', 'context')
- grad_gain_attn: float32 [512], replicated
- grad_qkv: float32 [512, 1536], replicated
- grad_out: float32 [512, 512], replicated
- grad_gain_mix: float32 [512], replicated
- grad_control: float32 [512, 8], replicated
- grad_in: float32 [8, 512, 2048], P('expert')
- grad_back: float32 [8, 2048, 512], P('expert')
- stats: float32 [3], replicated
Inputs may be any that keep to these rules, and one draw needn't show every extreme that they name: `segments`: never falling along a sequence, starting at 0. Along each sequence the valid slots are the leading ones, and the empty slots after them lie in the sequence's last document; in each replica some sequence is valid in all 1024 slots.
All inputs are finite; a program needn't handle non-finite values.
Results may differ from a plain program's by a relative error of at most 0.033.
Values may be sent and summed in bfloat16 or wider, within the bound.
A program may use at most 448 MiB of HBM per device.

v0:
```python
import jax
import jax.numpy as jnp
from jax import lax
from jax.sharding import PartitionSpec as P

HEADS = 8


NEG_FILL = -1e30


def shifted(x, axis, by):
    peers = lax.axis_size(axis)
    pairs = [(i, i + by) for i in range(peers) if 0 <= i + by < peers]
    return lax.ppermute(x, axis, pairs)


def joined_2(x, axis, combine):
    everything = jax.tree.map(
        lambda part, kind: lax.all_gather(part.astype(kind), axis), x, (jnp.bfloat16, jnp.bfloat16)
    )

    def take(k):
        return jax.tree.map(lambda part, own: part[k].astype(own.dtype), everything, x)

    return lax.fori_loop(
        1, lax.axis_size(axis), lambda k, so_far: combine(so_far, take(k)), take(0)
    )


def layer_norm(stream, gain):
    center = stream - jnp.mean(stream, -1, keepdims=True)
    spread = jnp.mean(center * center, -1, keepdims=True)
    return center * lax.rsqrt(spread + 1e-05) * gain


def merge_softmax(first, second):
    larger = jnp.maximum(first[0], second[0])
    summed = first[1] * jnp.exp(first[0] - larger) + second[1] * jnp.exp(second[0] - larger)
    return (larger, summed)


def per_device(
    tokens,
    gain_attn,
    query_key_value_weight,
    w_out,
    gain_mix,
    w_control,
    w_in,
    w_back,
    segments,
    valid,
    cotangent,
):
    rep_count, seq_count, pos_len, model_width = tokens.shape
    head_count = HEADS
    head_size = model_width // head_count
    score_scale = head_size ** (-0.5)
    item_count = rep_count * seq_count
    context_id = lax.axis_index("context")

    def key_allowed(seg_full, valid_full):
        steps_here = jnp.arange(pos_len, dtype=jnp.int32)
        query_place = context_id * pos_len + steps_here
        key_place = jnp.concatenate(((context_id - 1) * pos_len + steps_here, query_place))
        seg_query = lax.dynamic_slice_in_dim(seg_full, context_id * pos_len, pos_len)
        earlier_start = jnp.maximum(context_id - 1, 0) * pos_len
        seg_keys = jnp.concatenate(
            (lax.dynamic_slice_in_dim(seg_full, earlier_start, pos_len), seg_query)
        )
        valid_here = lax.dynamic_slice_in_dim(valid_full, context_id * pos_len, pos_len)
        valid_keys = jnp.concatenate(
            (lax.dynamic_slice_in_dim(valid_full, earlier_start, pos_len), valid_here)
        )
        return (
            (key_place[None, :] <= query_place[:, None])
            & (key_place[None, :] >= 0)
            & (seg_keys[None, :] == seg_query[:, None])
            & (valid_keys[None, :] > 0)
        )

    def masked_scores(query, keys, seg_full, valid_full):
        scores = (
            jnp.einsum("qhd,khd->hqk", query, keys, preferred_element_type=jnp.float32)
            * score_scale
        )
        return jnp.where(key_allowed(seg_full, valid_full)[None], scores, NEG_FILL)

    def attend_forward(pack):
        query, keys, values, seg_full, valid_full = pack
        scores = masked_scores(query, keys, seg_full, valid_full)
        biggest_entry = jnp.max(scores, -1, keepdims=True)
        log_sums = biggest_entry + jnp.log(
            jnp.sum(jnp.exp(scores - biggest_entry), -1, keepdims=True)
        )
        probs_low = jnp.exp(scores - log_sums).astype(jnp.bfloat16)
        attended = jnp.einsum("hqk,khd->qhd", probs_low, values, preferred_element_type=jnp.float32)
        return (attended.reshape(pos_len, model_width).astype(jnp.bfloat16), log_sums[..., 0])

    def attend_backward(pack):
        query, keys, values, seg_full, valid_full, log_sums, d_att = pack
        scores = masked_scores(query, keys, seg_full, valid_full)
        probs = jnp.exp(scores - log_sums[..., None])
        probs_low = probs.astype(jnp.bfloat16)
        d_probs = jnp.einsum("qhd,khd->hqk", d_att, values, preferred_element_type=jnp.float32)
        row_dot = jnp.sum(probs * d_probs, -1, keepdims=True)
        d_scores = (probs * (d_probs - row_dot)).astype(jnp.bfloat16)
        d_query = (
            jnp.einsum("hqk,khd->qhd", d_scores, keys, preferred_element_type=jnp.float32)
            * score_scale
        )
        d_keys = (
            jnp.einsum("hqk,qhd->khd", d_scores, query, preferred_element_type=jnp.float32)
            * score_scale
        )
        d_values = jnp.einsum("hqk,qhd->khd", probs_low, d_att, preferred_element_type=jnp.float32)
        return (d_query, d_keys, d_values)

    stream = tokens.astype(jnp.float32)
    normed, attn_norm_back = jax.vjp(layer_norm, stream, gain_attn)
    activation_reduced = normed.astype(jnp.bfloat16)
    qkv_low = jnp.dot(
        activation_reduced, query_key_value_weight, preferred_element_type=jnp.float32
    ).astype(jnp.bfloat16)
    key_value_pairs = qkv_low[..., model_width:]
    remote = shifted(key_value_pairs, "context", 1)
    joined = jnp.concatenate((remote, key_value_pairs), axis=2)
    queries = qkv_low[..., :model_width].reshape(item_count, pos_len, head_count, head_size)
    keys_all = joined[..., :model_width].reshape(item_count, 2 * pos_len, head_count, head_size)
    values_all = joined[..., model_width:].reshape(item_count, 2 * pos_len, head_count, head_size)
    seg_items = segments.reshape(item_count, -1)
    valid_items = valid.reshape(item_count, -1)
    attended, log_sums = lax.map(
        attend_forward, (queries, keys_all, values_all, seg_items, valid_items)
    )
    attended = attended.reshape(rep_count, seq_count, pos_len, model_width)
    attn_out = jnp.dot(attended, w_out, preferred_element_type=jnp.float32)
    resid = stream + attn_out
    normed_mix, mix_norm_back = jax.vjp(layer_norm, resid, gain_mix)
    u_low = normed_mix.astype(jnp.bfloat16)
    logits = jnp.dot(u_low, w_control, preferred_element_type=jnp.float32)
    here_valid = lax.dynamic_slice_in_dim(valid, context_id * pos_len, pos_len, 2) > 0
    masked = jnp.where(here_valid[..., None], logits, NEG_FILL)
    top_local = jnp.max(masked, 1)
    total_local = jnp.sum(jnp.exp(masked - top_local[:, None]), 1)
    group_top, group_total = joined_2((top_local, total_local), "expert", merge_softmax)
    weights = jnp.exp(masked - group_top[:, None]) / group_total[:, None]
    weights_low = weights.astype(jnp.bfloat16)
    part_weights = weights_low
    mixed = lax.psum_scatter(
        jnp.einsum(
            "rspe,rspd->erpd", part_weights, u_low, preferred_element_type=jnp.float32
        ).astype(jnp.bfloat16),
        "expert",
        scatter_dimension=0,
        tiled=True,
    )
    pre_act = jnp.einsum("erpd,edf->erpf", mixed, w_in, preferred_element_type=jnp.float32)
    activated, gelu_back = jax.vjp(jax.nn.gelu, pre_act)
    act_low = activated.astype(jnp.bfloat16)
    expert_low = jnp.einsum(
        "erpf,efd->erpd", act_low, w_back, preferred_element_type=jnp.float32
    ).astype(jnp.bfloat16)
    outs_all = lax.all_gather(expert_low, "expert", axis=0, tiled=True)
    mix_out = jnp.einsum(
        "rspe,erpd->rspd", weights_low, outs_all, preferred_element_type=jnp.float32
    )
    out_full = resid + mix_out
    part_weights = weights_low
    d_expert = lax.psum_scatter(
        jnp.einsum(
            "rspe,rspd->erpd", part_weights, cotangent, preferred_element_type=jnp.float32
        ).astype(jnp.bfloat16),
        "expert",
        scatter_dimension=0,
        tiled=True,
    )
    grad_back = jnp.einsum("erpf,erpd->efd", act_low, d_expert, preferred_element_type=jnp.float32)
    d_act = jnp.einsum("erpd,efd->erpf", d_expert, w_back, preferred_element_type=jnp.float32)
    d_pre_low = gelu_back(d_act)[0].astype(jnp.bfloat16)
    grad_in = jnp.einsum("erpd,erpf->edf", mixed, d_pre_low, preferred_element_type=jnp.float32)
    d_mixed_low = jnp.einsum(
        "erpf,edf->erpd", d_pre_low, w_in, preferred_element_type=jnp.float32
    ).astype(jnp.bfloat16)
    mixed_all = lax.all_gather(d_mixed_low, "expert", axis=0, tiled=True)
    d_weights = jnp.einsum(
        "rspd,erpd->rspe", cotangent, outs_all, preferred_element_type=jnp.float32
    ) + jnp.einsum("rspd,erpd->rspe", u_low, mixed_all, preferred_element_type=jnp.float32)
    group_dot = lax.psum(jnp.sum(weights * d_weights, 1).astype(jnp.bfloat16), "expert").astype(
        jnp.float32
    )
    d_logits_low = (weights * (d_weights - group_dot[:, None])).astype(jnp.bfloat16)
    grad_control = jnp.einsum(
        "rspd,rspe->de", u_low, d_logits_low, preferred_element_type=jnp.float32
    )
    d_u = jnp.dot(d_logits_low, w_control.T, preferred_element_type=jnp.float32) + jnp.einsum(
        "rspe,erpd->rspd", weights_low, mixed_all, preferred_element_type=jnp.float32
    )
    d_resid_norm, grad_gain_mix = mix_norm_back(d_u)
    d_resid = cotangent.astype(jnp.float32) + d_resid_norm
    d_attn_low = d_resid.astype(jnp.bfloat16)
    grad_out = jnp.einsum("rspd,rspe->de", attended, d_attn_low, preferred_element_type=jnp.float32)
    d_attended = jnp.dot(d_attn_low, w_out.T, preferred_element_type=jnp.float32).astype(
        jnp.bfloat16
    )
    d_attended = d_attended.reshape(item_count, pos_len, head_count, head_size)
    d_query, d_keys, d_values = lax.map(
        attend_backward,
        (queries, keys_all, values_all, seg_items, valid_items, log_sums, d_attended),
    )
    d_query = d_query.reshape(rep_count, seq_count, pos_len, model_width)
    d_keys = d_keys.reshape(rep_count, seq_count, 2 * pos_len, model_width)
    d_values = d_values.reshape(rep_count, seq_count, 2 * pos_len, model_width)
    sent_back = jnp.concatenate((d_keys[:, :, :pos_len], d_values[:, :, :pos_len]), -1)
    returned = shifted(sent_back.astype(jnp.bfloat16), "context", -1).astype(sent_back.dtype)
    d_keys_vals = jnp.concatenate((d_keys[:, :, pos_len:], d_values[:, :, pos_len:]), -1) + returned
    d_qkv_low = jnp.concatenate((d_query, d_keys_vals), -1).astype(jnp.bfloat16)
    grad_qkv = jnp.einsum(
        "rspd,rspc->dc", activation_reduced, d_qkv_low, preferred_element_type=jnp.float32
    )
    d_normed = jnp.dot(d_qkv_low, query_key_value_weight.T, preferred_element_type=jnp.float32)
    d_stream_norm, grad_gain_attn = attn_norm_back(d_normed)
    d_tokens = (d_resid + d_stream_norm).astype(jnp.bfloat16)
    valid_float = here_valid.astype(jnp.float32)[..., None]
    square_sums = jnp.stack(
        [
            jnp.sum(valid_float * out_full * out_full),
            jnp.sum(valid_float * attn_out * attn_out),
            jnp.sum(valid_float * mix_out * mix_out),
            jnp.sum(valid_float),
        ]
    )
    grad_in, grad_back = (
        lax.psum(grad_in.astype(jnp.bfloat16), ("context", "dp")).astype(jnp.float32),
        lax.psum(grad_back.astype(jnp.bfloat16), ("context", "dp")).astype(jnp.float32),
    )
    grad_gain_attn, grad_qkv, grad_out, grad_gain_mix, grad_control, square_sums = lax.psum(
        (grad_gain_attn, grad_qkv, grad_out, grad_gain_mix, grad_control, square_sums),
        ("expert", "context", "dp"),
    )
    stats = jnp.sqrt(square_sums[:3] / (square_sums[3] * model_width))
    return (
        out_full.astype(jnp.bfloat16),
        d_tokens,
        grad_gain_attn,
        grad_qkv,
        grad_out,
        grad_gain_mix,
        grad_control,
        grad_in,
        grad_back,
        stats,
    )


def solution(mesh):
    in_specs = (
        P("dp", "expert", "context", None),
        P(),
        P(),
        P(),
        P(),
        P(),
        P("expert", None, None),
        P("expert", None, None),
        P("dp", "expert", None),
        P("dp", "expert", None),
        P("dp", "expert", "context", None),
    )
    out_specs = (
        P("dp", "expert", "context", None),
        P("dp", "expert", "context", None),
        P(),
        P(),
        P(),
        P(),
        P(),
        P("expert", None, None),
        P("expert", None, None),
        P(),
    )
    return jax.shard_map(
        per_device, mesh=mesh, in_specs=in_specs, out_specs=out_specs, check_vma=False
    )
```

profile of v0, /device:TPU:0, one launch (start us, length us, event | category | flops | bytes accessed | tf_op | source)
XLA Modules:
  0.0 1072.8 jit_solution(4460624790265613192)
XLA Ops:
  25.6 7.4 collective-permute-start
  40.9 79.8 %collective-permute-done = bf16[2,2,512,1024]{3,2,1,0:T(8,128)(2,1)} collective-permute-done((bf16[2,2,512,1024]{3,2,1,0:T(8,128)(2,1)}, bf16[2,2,512,1024]{3,2,1,0:T(8,128)(2,1)}, u32[]{:S(2)}, u32[]{:S(2)}) %collective-permute-start) | collective-permute-done | bytes 4194336 | tf_op jit(solution)/shard_map/ppermute | solution.py:15
  126.6 6.3 copy.106
  132.8 6.3 copy.104
  139.1 68.6 %while.49 = (s32[]{:T(128)}, bf16[4,512,512]{1,2,0:T(8,128)(2,1)}, f32[4,8,512]{2,1,0:T(8,128)}, bf16[4,1024,8,64]{1,3,2,0:T(8,128)(2,1)}, s32[]{:T(128)}, /*ind...) while((s32[]{:T(128)}, bf16[4,512,512]{1,2,0:T(8,128)(2,1)}, ...), condition=%wide.region_5.6_spmd, body=%wide.region_2.5_spmd.sunk | while | flops 1122765824 | bytes 56816836 | solution.py:134
  207.7 6.3 fusion.113
  217.8 6.2 copy.110
  237.3 7.6 convert_bitcast_fusion.1
  244.9 9.7 copy.112
  254.7 7.2 convert_bitcast_fusion
  261.8 11.1 %copy.121 = bf16[8,2,512,512]{3,2,1,0:T(8,128)(2,1)} copy(bf16[8,2,512,512]{3,0,2,1:T(8,128)(2,1)} %convert_bitcast_fusion) | data formatting | bytes 16777216 | tf_op jit(solution)/shard_map/convert_element_type | solution.py:174
  273.5 55.3 %reduce-scatter.3.cloned.1.call-done = bf16[2,2,512,512]{3,2,1,0:T(8,128)(2,1)} async-done(((bf16[8,2,512,512]{3,2,1,0:T(8,128)(2,1)}), bf16[2,2,512,512]{3,2,1,0:T(8,128)(2,1)}) %reduce-scatter.3.cloned.1.call-update) | async-done | bytes 2097168 | tf_op jit(solution)/shard_map/reduce_scatter | solution.py:151
  328.8 7.1 fusion.76
  335.9 9.2 copy-done.42
  345.1 6.7 fusion.85
  351.8 51.4 %reduce-scatter.5.cloned.1.call-done = bf16[2,2,512,512]{3,2,1,0:T(8,128)(2,1)} async-done(((bf16[8,2,512,512]{3,2,1,0:T(8,128)(2,1)}), bf16[2,2,512,512]{3,2,1,0:T(8,128)(2,1)}) %reduce-scatter.5.cloned.1.call-update) | async-done | bytes 2097168 | tf_op jit(solution)/shard_map/reduce_scatter | solution.py:171
  403.2 19.8 %fusion.50 = bf16[2,2,512,2048]{3,2,1,0:T(8,128)(2,1)} fusion(f32[2,2,512,2048]{3,2,1,0:T(8,128)} %copy-done.42, bf16[2,2,512,512]{3,2,1,0:T(8,128)(2,1)} %reduce-scatter.5.cloned.1.call-done, bf16[2,2048,512]{2,1,0:T(8,128)(2,1)} %param.24), kind=kOutput, calls=%fused_computation.79 | convolution fusion | flops 4378853376 | bytes 31457280 | tf_op jit(solution)/shard_map/erpd,efd->erpf/dot_general | solution.py:180
  423.0 9.6 fusion.88
  437.0 10.7 bitcast_convert_fusion.1
  447.7 11.7 %bitcast_convert_fusion = bf16[2,2048,512]{2,1,0:T(8,128)(2,1)} fusion(bf16[2,2,512,512]{3,2,1,0:T(8,128)(2,1)S(1)} %copy-done.41, f32[2,2,512,2048]{3,2,1,0:T(8,128)} %copy-done.42), kind=kOutput, calls=%fused_computation.85 | convolution fusion | flops 4334813184 | bytes 23068672 | tf_op jit(solution)/shard_map/erpf,erpd->efd/dot_general | solution.py:179
  463.7 10.9 %fusion.56 = f32[2,512,8,2]{2,3,1,0:T(2,128)S(1)} fusion(bf16[8,2,512,512]{3,2,1,0:T(8,128)(2,1)} %all-gather.5.cloned.1.call-done, bf16[2,2,512,512]{3,2,1,0:T(8,128)(2,1)} %param.27), kind=kOutput, calls=%fused_computation.93 | convolution fusion | flops 16777216 | bytes 10551296 | tf_op jit(solution)/shard_map/rspd,erpd->rspe/dot_general | solution.py:187
  475.5 11.9 %fusion.58 = f32[2,512,512,2]{2,3,1,0:T(2,128)} fusion(bf16[2,2,512,8]{3,1,2,0:T(2,128)(2,1)S(1)} %copy.111, bf16[8,2,512,512]{3,2,1,0:T(8,128)(2,1)} %all-gather.5.cloned.1.call-done), kind=kOutput, calls=%fused_computation.95 | convolution fusion | flops 16777216 | bytes 12615680 | tf_op jit(solution)/shard_map/rspe,erpd->rspd/dot_general | solution.py:166
  487.4 7.2 copy.115
  494.6 28.8 %all-gather.7.cloned.1.call-done = bf16[8,2,512,512]{3,2,1,0:T(8,128)(2,1)} async-done(((bf16[2,2,512,512]{3,2,1,0:T(8,128)(2,1)}), bf16[8,2,512,512]{3,2,1,0:T(8,128)(2,1)}) %all-gather.7.cloned.1.call-update) | async-done | bytes 8388624 | tf_op jit(solution)/shard_map/all_gather | solution.py:186
  523.5 10.5 fusion.54
  534.6 11.1 %fusion.52 = f32[2,512,512,2]{2,3,1,0:T(2,128)} fusion(bf16[2,2,512,8]{3,1,2,0:T(2,128)(2,1)S(1)} %copy.111, bf16[8,2,512,512]{3,2,1,0:T(8,128)(2,1)} %all-gather.7.cloned.1.call-done), kind=kOutput, calls=%fused_computation.89 | convolution fusion | flops 16777216 | bytes 12615680 | tf_op jit(solution)/shard_map/rspe,erpd->rspd/dot_general | solution.py:197
  545.6 7.2 copy.128
  552.9 11.1 %psum.63 = bf16[2,512,8]{1,2,0:T(8,128)(2,1)S(1)} all-reduce(bf16[2,512,8]{1,2,0:T(8,128)(2,1)S(1)} %fusion.102), channel_id=1, replica_groups=mesh['expert'=4,'context'=2,'dp'=4] {'expert'}, use_global_device_ids=true, to_apply=%region_15.16 | all-reduce | flops 8192 | bytes 32768 | tf_op jit(solution)/shard_map/psum | solution.py:190
  564.1 9.3 fusion.70
  579.2 215.1 %while.51 = (s32[]{:T(128)}, bf16[4,512,8,64]{1,3,2,0:T(8,128)(2,1)}, f32[4,1024,8,64]{1,3,2,0:T(8,128)}, f32[4,1024,8,64]{1,3,2,0:T(8,128)}, bf16[4,1024,8,64]{...) while((s32[]{:T(128)}, ...), condition=%wide.region_20.21_spmd, body=%wide.region_18.20_spmd.sunk | while | flops 2725514240 | bytes 204621056 | solution.py:208
  582.0 9.5 fusion.170
  591.5 12.9 %multiply_reduce_fusion.5 = (f32[8,512]{1,0:T(8,128)S(1)}, f32[8,512,1024]{2,1,0:T(8,128)}) fusion(f32[8,512,1024]{2,1,0:T(8,128)} %fusion.170, f32[8,512]{1,0:T(8,128)S(1)} %dynamic-slice_bitcast_fusion.2, bf16[4,1024,8,64]{1,3,2,0:T(8,128)(2,1)} %get-tuple-element.1132, s32[]{:T(128)S(6)} %copy.204, ...), kind=kOutput, calls=%fused_computation.34.clone.1 | convolution fusion | flops 557838336 | bytes 35685376 | tf_op jit(solution)/shard_map/while/body/eval_jaxpr/qhd,khd->hqk/dot_general | solution.py:85
  604.5 11.8 %multiply_convert_fusion.6 = bf16[8,512,1024]{2,1,0:T(8,128)(2,1)S(1)} fusion(f32[8,512,1024]{2,1,0:T(8,128)} %get-tuple-element.1021, f32[8,512,1024]{2,1,0:T(8,128)} %fusion.170, f32[8,512]{1,0:T(8,128)S(1)} %get-tuple-element.1022), kind=kLoop, calls=%fused_computation.33.clone.1 | loop fusion | flops 12582912 | bytes 41959424 | tf_op jit(solution)/shard_map/while/body/eval_jaxpr/convert_element_type | solution.py:108
  635.3 9.5 fusion.170
  644.8 12.9 %multiply_reduce_fusion.5 = (f32[8,512]{1,0:T(8,128)S(1)}, f32[8,512,1024]{2,1,0:T(8,128)}) fusion(f32[8,512,1024]{2,1,0:T(8,128)} %fusion.170, f32[8,512]{1,0:T(8,128)S(1)} %dynamic-slice_bitcast_fusion.2, bf16[4,1024,8,64]{1,3,2,0:T(8,128)(2,1)} %get-tuple-element.1132, s32[]{:T(128)S(6)} %copy.204, ...), kind=kOutput, calls=%fused_computation.34.clone.1 | convolution fusion | flops 557838336 | bytes 35685376 | tf_op jit(solution)/shard_map/while/body/eval_jaxpr/qhd,khd->hqk/dot_general | solution.py:85
  657.7 11.8 %multiply_convert_fusion.6 = bf16[8,512,1024]{2,1,0:T(8,128)(2,1)S(1)} fusion(f32[8,512,1024]{2,1,0:T(8,128)} %get-tuple-element.1021, f32[8,512,1024]{2,1,0:T(8,128)} %fusion.170, f32[8,512]{1,0:T(8,128)S(1)} %get-tuple-element.1022), kind=kLoop, calls=%fused_computation.33.clone.1 | loop fusion | flops 12582912 | bytes 41959424 | tf_op jit(solution)/shard_map/while/body/eval_jaxpr/convert_element_type | solution.py:108
  689.3 9.5 fusion.170
  698.8 13.8 %multiply_reduce_fusion.5 = (f32[8,512]{1,0:T(8,128)S(1)}, f32[8,512,1024]{2,1,0:T(8,128)}) fusion(f32[8,512,1024]{2,1,0:T(8,128)} %fusion.170, f32[8,512]{1,0:T(8,128)S(1)} %dynamic-slice_bitcast_fusion.2, bf16[4,1024,8,64]{1,3,2,0:T(8,128)(2,1)} %get-tuple-element.1132, s32[]{:T(128)S(6)} %copy.204, ...), kind=kOutput, calls=%fused_computation.34.clone.1 | convolution fusion | flops 557838336 | bytes 35685376 | tf_op jit(solution)/shard_map/while/body/eval_jaxpr/qhd,khd->hqk/dot_general | solution.py:85
  712.6 11.6 %multiply_convert_fusion.6 = bf16[8,512,1024]{2,1,0:T(8,128)(2,1)S(1)} fusion(f32[8,512,1024]{2,1,0:T(8,128)} %get-tuple-element.1021, f32[8,512,1024]{2,1,0:T(8,128)} %fusion.170, f32[8,512]{1,0:T(8,128)S(1)} %get-tuple-element.1022), kind=kLoop, calls=%fused_computation.33.clone.1 | loop fusion | flops 12582912 | bytes 41959424 | tf_op jit(solution)/shard_map/while/body/eval_jaxpr/convert_element_type | solution.py:108
  743.2 9.8 fusion.170
  753.0 13.2 %multiply_reduce_fusion.5 = (f32[8,512]{1,0:T(8,128)S(1)}, f32[8,512,1024]{2,1,0:T(8,128)}) fusion(f32[8,512,1024]{2,1,0:T(8,128)} %fusion.170, f32[8,512]{1,0:T(8,128)S(1)} %dynamic-slice_bitcast_fusion.2, bf16[4,1024,8,64]{1,3,2,0:T(8,128)(2,1)} %get-tuple-element.1132, s32[]{:T(128)S(6)} %copy.204, ...), kind=kOutput, calls=%fused_computation.34.clone.1 | convolution fusion | flops 557838336 | bytes 35685376 | tf_op jit(solution)/shard_map/while/body/eval_jaxpr/qhd,khd->hqk/dot_general | solution.py:85
  766.2 11.6 %multiply_convert_fusion.6 = bf16[8,512,1024]{2,1,0:T(8,128)(2,1)S(1)} fusion(f32[8,512,1024]{2,1,0:T(8,128)} %get-tuple-element.1021, f32[8,512,1024]{2,1,0:T(8,128)} %fusion.170, f32[8,512]{1,0:T(8,128)S(1)} %get-tuple-element.1022), kind=kLoop, calls=%fused_computation.33.clone.1 | loop fusion | flops 12582912 | bytes 41959424 | tf_op jit(solution)/shard_map/while/body/eval_jaxpr/convert_element_type | solution.py:108
  816.4 7.7 convert_element_type.219
  862.7 46.1 %collective-permute-done.1 = bf16[2,2,512,1024]{3,2,1,0:T(8,128)(2,1)} collective-permute-done((bf16[2,2,512,1024]{3,2,1,0:T(8,128)(2,1)}, bf16[2,2,512,1024]{3,2,1,0:T(8,128)(2,1)}, u32[]{:S(2)}, u32[]{:S(2)}) %collective-permute-start.1) | collective-permute-done | bytes 4194336 | tf_op jit(solution)/shard_map/ppermute | solution.py:15
  919.3 7.1 fusion.69
  928.4 40.0 %all-reduce = (f32[512]{0:T(512)}, f32[512]{0:T(512)}, f32[512,8]{0,1:T(8,128)}, f32[4]{0:T(128)S(1)}) all-reduce(f32[512]{0:T(512)S(1)} %get-tuple-element.670, f32[512]{0:T(512)S(1)} %copy-done.38, f32[512,8]{0,1:T(8,128)S(1)} %convolution_bitcast_fusion.1, ...), channel_id=1, replica_groups=mesh['expert'=4,'context'=2,'dp'=4] {'expert','context','dp'}, use_global_device_ids=true, to_apply=%region_24.25 | all-reduce | flops 5124 | bytes 40992 | tf_op jit(solution)/shard_map/psum | solution.py:238
  969.0 6.6 add_convert_fusion
  980.9 80.0 %all-reduce.6.cloned.1.call-done = (f32[512,1536]{1,0:T(8,128)}, f32[512,512]{1,0:T(8,128)}) async-done(((f32[512,1536]{1,0:T(8,128)}, f32[512,512]{1,0:T(8,128)}), (f32[512,1536]{1,0:T(8,128)}, f32[512,512]{1,0:T(8,128)})) %all-reduce.6.cloned.1.call-update) | async-done | bytes 4194320 | tf_op jit(solution)/shard_map/psum | solution.py:238
  (280 shorter events, 293.8 us)
Async XLA Ops:
  7.2 9.2 copy-start
  7.2 9.1 copy-start.36
  7.2 321.5 %reduce-scatter.3.cloned.1.call-start = ((), (), s32[]{:S(2)}) async-start(), calls=%async_computation.2 | async-start | bytes 10485760 | tf_op jit(solution)/shard_map/reduce_scatter | solution.py:151
  11.5 4.9 copy-start.4
  13.5 6.8 copy-start.24
  16.4 4.0 copy-start.26
  20.3 2.7 copy-start.12
  25.6 10.5 copy-start.35
  25.6 10.5 copy-start.32
  25.6 95.1 %collective-permute-start = (bf16[2,2,512,1024]{3,2,1,0:T(8,128)(2,1)}, bf16[2,2,512,1024]{3,2,1,0:T(8,128)(2,1)}, u32[]{:S(2)}, u32[]{:S(2)}) collective-permute-start(bf16[2,2,512,1024]{3,2,1,0:T(8,128)(2,1)} %slice.52), channel_id=1, source_target_pairs={{0,4},{1,5},{2,6},{3,7},{8,12},{9,13},{10,14},{11,15},{16,20},{17,... | collective-permute-start | bytes 12582920 | tf_op jit(solution)/shard_map/ppermute | solution.py:15
  139.1 68.6 %copy-start.18 = (bf16[512,512]{1,0:T(8,128)(2,1)S(1)}, bf16[512,512]{1,0:T(8,128)(2,1)}, u32[]{:S(2)}) copy-start(bf16[512,512]{1,0:T(8,128)(2,1)} %param.20) | copy-start | bytes 1572868
  207.7 6.3 copy-start.22
  207.7 6.3 copy-start.23
  216.0 8.0 copy-start.33
  254.6 148.6 %reduce-scatter.5.cloned.1.call-start = ((), (), s32[]{:S(2)}) async-start(), calls=%async_computation.4 | async-start | bytes 10485760 | tf_op jit(solution)/shard_map/reduce_scatter | solution.py:171
  273.0 190.7 %all-gather.5.cloned.1.call-start = ((), (), s32[]{:S(2)}) async-start(), calls=%async_computation.3 | async-start | bytes 10485760 | tf_op jit(solution)/shard_map/all_gather | solution.py:165
  328.8 16.3 %copy-start.39 = (bf16[2,2048,512]{2,1,0:T(8,128)(2,1)S(1)}, bf16[2,2048,512]{2,1,0:T(8,128)(2,1)}, u32[]{:S(2)}) copy-start(bf16[2,2048,512]{2,1,0:T(8,128)(2,1)} %param.24) | copy-start | bytes 12582916
  335.8 9.2 copy-start.42
  351.8 171.7 %all-gather.7.cloned.1.call-start = ((), (), s32[]{:S(2)}) async-start(), calls=%async_computation.5 | async-start | bytes 10485760 | tf_op jit(solution)/shard_map/all_gather | solution.py:186
  403.2 19.8 %copy-start.40 = (bf16[2,512,2048]{2,1,0:T(8,128)(2,1)S(1)}, bf16[2,512,2048]{2,1,0:T(8,128)(2,1)}, u32[]{:S(2)}) copy-start(bf16[2,512,2048]{2,1,0:T(8,128)(2,1)} %param.23) | copy-start | bytes 12582916
  432.6 383.7 %all-reduce.8.cloned.1.call-start = ((), (), s32[]{:S(2)}) async-start(), calls=%async_computation.7 | async-start | bytes 16777216 | tf_op jit(solution)/shard_map/psum | solution.py:235
  437.0 10.7 copy-start.41
  459.4 601.5 %all-reduce.6.cloned.1.call-start = ((), (), s32[]{:S(2)}) async-start(), calls=%async_computation.6 | async-start | bytes 8388608 | tf_op jit(solution)/shard_map/psum | solution.py:238
  564.1 9.3 copy-start.20
  564.1 9.3 copy-start.3
  576.7 2.6 copy-start.15
  604.4 15.8 %copy-start.1 = (f32[8,512,1024]{2,1,0:T(8,128)S(1)}, f32[8,512,1024]{2,1,0:T(8,128)}, u32[]{:S(2)}) copy-start(f32[8,512,1024]{2,1,0:T(8,128)} %get-tuple-element.1021) | copy-start | bytes 50331652 | tf_op jit(solution)/shard_map/while
  657.7 16.6 %copy-start.1 = (f32[8,512,1024]{2,1,0:T(8,128)S(1)}, f32[8,512,1024]{2,1,0:T(8,128)}, u32[]{:S(2)}) copy-start(f32[8,512,1024]{2,1,0:T(8,128)} %get-tuple-element.1021) | copy-start | bytes 50331652 | tf_op jit(solution)/shard_map/while
  712.6 15.6 %copy-start.1 = (f32[8,512,1024]{2,1,0:T(8,128)S(1)}, f32[8,512,1024]{2,1,0:T(8,128)}, u32[]{:S(2)}) copy-start(f32[8,512,1024]{2,1,0:T(8,128)} %get-tuple-element.1021) | copy-start | bytes 50331652 | tf_op jit(solution)/shard_map/while
  766.1 15.6 %copy-start.1 = (f32[8,512,1024]{2,1,0:T(8,128)S(1)}, f32[8,512,1024]{2,1,0:T(8,128)}, u32[]{:S(2)}) copy-start(f32[8,512,1024]{2,1,0:T(8,128)} %get-tuple-element.1021) | copy-start | bytes 50331652 | tf_op jit(solution)/shard_map/while
  814.9 93.9 %collective-permute-start.1 = (bf16[2,2,512,1024]{3,2,1,0:T(8,128)(2,1)}, bf16[2,2,512,1024]{3,2,1,0:T(8,128)(2,1)}, u32[]{:S(2)}, u32[]{:S(2)}) collective-permute-start(bf16[2,2,512,1024]{3,2,1,0:T(8,128)(2,1)} %pad_maximum_fusion.2), channel_id=1, source_target_pairs={{4,0},{5,1},{6,2},{7,3},{12,8},{13,9},{14,10},{15,11},{20,16},{21,... | collective-permute-start | bytes 12582920 | tf_op jit(solution)/shard_map/ppermute | solution.py:15
  816.4 7.7 copy-start.13
  816.4 13.2 %slice-start = ((s8[8388608]{0:T(1024)(128)(4,1)}), s8[4194304]{0:T(1024)(128)(4,1)S(1)}, s32[]{:S(2)}) async-start(s8[8388608]{0:T(1024)(128)(4,1)} %bitcast.257), calls=%async_computation.8 | async-start | bytes 8388608
  816.4 15.5 %slice-start.2 = ((s8[8388608]{0:T(1024)(128)(4,1)}), s8[4194304]{0:T(1024)(128)(4,1)S(1)}, s32[]{:S(2)}) async-start(s8[8388608]{0:T(1024)(128)(4,1)} %bitcast.261), calls=%async_computation.10 | async-start | bytes 8388608
  824.0 5.5 slice-start.1
  824.1 7.9 slice-start.3
  849.0 6.8 copy-start.21
  858.0 50.7 %copy-start.10 = (f32[2,2,512,512]{3,2,1,0:T(8,128)S(1)}, f32[2,2,512,512]{3,2,1,0:T(8,128)}, u32[]{:S(2)}) copy-start(f32[2,2,512,512]{3,2,1,0:T(8,128)} %copy.162) | copy-start | bytes 12582916
  858.0 50.7 %copy-start.11 = (f32[2,2,512,512]{3,2,1,0:T(8,128)S(1)}, f32[2,2,512,512]{3,2,1,0:T(8,128)}, u32[]{:S(2)}) copy-start(f32[2,2,512,512]{3,2,1,0:T(8,128)} %copy.161) | copy-start | bytes 12582916
  862.7 51.4 %copy-start.5 = (bf16[2,2,512,512]{2,3,1,0:T(8,128)(2,1)S(1)}, bf16[2,2,512,512]{2,3,1,0:T(8,128)(2,1)}, u32[]{:S(2)}) copy-start(bf16[2,2,512,512]{2,3,1,0:T(8,128)(2,1)} %copy.102) | copy-start | bytes 6291460
  862.7 51.4 %copy-start.16 = (bf16[2,2,512,512]{3,2,1,0:T(8,128)(2,1)S(1)}, bf16[2,2,512,512]{3,2,1,0:T(8,128)(2,1)}, u32[]{:S(2)}) copy-start(bf16[2,2,512,512]{3,2,1,0:T(8,128)(2,1)} %copy.134) | copy-start | bytes 6291460
  862.7 51.4 %copy-start.25 = (f32[2,2,512]{2,1,0:T(2,128)S(1)}, f32[2,2,512]{2,1,0:T(2,128)}, u32[]{:S(2)}) copy-start(f32[2,2,512]{2,1,0:T(2,128)} %copy-done.24) | copy-start | bytes 24580
  862.7 51.4 %copy-start.27 = (f32[2,2,512]{2,1,0:T(2,128)S(1)}, f32[2,2,512]{2,1,0:T(2,128)}, u32[]{:S(2)}) copy-start(f32[2,2,512]{2,1,0:T(2,128)} %copy-done.26) | copy-start | bytes 24580
  862.7 51.4 %copy-start.37 = (f32[512]{0:T(512)S(1)}, f32[512]{0:T(512)}, u32[]{:S(2)}) copy-start(f32[512]{0:T(512)} %param.18) | copy-start | bytes 6148
  919.3 7.1 copy-start.31
  919.3 7.2 copy-start.6
  926.4 42.5 %copy-start.29 = (f32[2,2,512]{2,1,0:T(2,128)S(1)}, f32[2,2,512]{2,1,0:T(2,128)}, u32[]{:S(2)}) copy-start(f32[2,2,512]{2,1,0:T(2,128)} %copy-done.28) | copy-start | bytes 24580
  1060.9 3.8 copy-start.17
  (10 other events, 17.5 us)
Sparse Core Ops, SparseCore 0:
  254.7 73.9 reduce-scatter.2
  331.5 71.6 reduce-scatter.4
  405.4 58.2 all-gather.4
  465.1 58.2 all-gather.6
  527.4 271.1 all-reduce.7
  919.4 141.4 all-reduce.5
where the time goes:
time: 1080 us; the launch traced here: 1070 us
  matrix products  351 us (32%)
  waiting for transfers between devices  346 us (32%)
  local copies, waits for them, and re-layouts  167 us (15%)
  other arithmetic  121 us (11%)
  blocking collectives  61.7 us (6%)
  between operations  15.5 us (1%)
    ppermute x2, waiting for transfers between devices, shifted(): return lax.ppermute(x, axis, pairs)  126 us
    psum x1, waiting for transfers between devices, per_device(): lax.psum((grad_gain_attn, grad_qkv, grad_out, grad_gain_mix, grad_control...  80 us
    dot_general x8, matrix products, masked_scores(): jnp.einsum('qhd,khd->hqk', query, keys, preferred_element_type=jnp.float32)  72.3 us
    unnamed x102, local copies, waits for them, and re-layouts  57.4 us
    reduce_scatter x1, waiting for transfers between devices, per_device(): lax.psum_scatter(jnp.einsum('rspe,rspd->erpd', part_weights, u_low, prefe...  55.3 us
    reduce_scatter x1, waiting for transfers between devices, per_device(): lax.psum_scatter(jnp.einsum('rspe,rspd->erpd', part_weights, cotangent, p...  51.4 us
    convert_element_type x4, other arithmetic, attend_backward(): d_scores = (probs * (d_probs - row_dot)).astype(jnp.bfloat16)  46.8 us
    psum x1, blocking collectives, per_device(): lax.psum((grad_gain_attn, grad_qkv, grad_out, grad_gain_mix, grad_control...  40 us
  transfers between devices with their start and end apart: 8, of which 7 were waited for; matrix products, arithmetic and copies ran while one was open for 42% of the time, Pallas kernels for 0%

commit v1 on v0

v1 whole, which is shorter than its diff:
```python
import functools
import jax
import jax.numpy as jnp
from jax import lax
from jax.experimental import pallas as pl
from jax.experimental.pallas import tpu as pltpu
from jax.sharding import PartitionSpec as P

HEADS = 8
NEG_FILL = -1e30
MESH = pl.DeviceIdType.MESH
BF = jnp.bfloat16
F32 = jnp.float32
ANY = pl.BlockSpec(memory_space=pl.ANY)
VM = pl.BlockSpec(memory_space=pltpu.VMEM)
VMEM_LIMIT = 60 * 1024 * 1024


def dot(a, b, dims=((1,), (0,))):
    return lax.dot_general(a, b, (dims, ((), ())), preferred_element_type=F32)


def normalized(x):
    center = x - jnp.mean(x, -1, keepdims=True)
    spread = jnp.mean(center * center, -1, keepdims=True)
    rstd = lax.rsqrt(spread + 1e-05)
    return center * rstd, rstd


def ring(n_expert, n_context):
    e = lax.axis_index("expert")
    c = lax.axis_index("context")
    n = n_expert * n_context
    me = e * n_context + c

    def peer(k):
        j = lax.rem(me + k, n)
        pe = lax.div(j, n_context)
        pc = lax.rem(j, n_context)
        return j, pe, pc

    return e, c, me, n, peer


def enter(peer, n):
    barrier = pltpu.get_barrier_semaphore()
    for k in range(1, n):
        _, pe, pc = peer(k)
        pl.semaphore_signal(
            barrier, inc=1, device_id={"expert": pe, "context": pc}, device_id_type=MESH
        )
    pl.semaphore_wait(barrier, n - 1)


def mask_bias(bias, kmark, qmark, s, q0, qn):
    kk = q0 + qn
    place_k = lax.broadcasted_iota(jnp.int32, (kk, qn), 0)
    place_q = lax.broadcasted_iota(jnp.int32, (kk, qn), 1) + q0
    same = kmark[s, pl.ds(0, kk), :] == qmark[s, :, pl.ds(q0, qn)]
    bias[pl.ds(0, kk), :] = jnp.where(same & (place_k <= place_q), 0.0, NEG_FILL)


def forward_kernel(
    tokens, cot, kmark, qmark, gain, wqkv, wout,
    resid_m, cot_m, tok_a, qkv_o, att_o, lse_o, sq_o,
    tok, qkv, att, res, bias,
    tok_s, tok_r, cot_s, cot_r, res_s, res_r, own_s, save_s,
    *, n_expert, n_context,
):
    e, c, me, n, peer = ring(n_expert, n_context)
    seqs, length, width = qkv_o.shape[0], qkv_o.shape[1], tokens.shape[-1]
    half = length // n_context
    slab = half // n_expert
    qn = 256
    enter(peer, n)
    outgoing = []
    for s in range(seqs):
        for k in range(1, n_context):
            pc = lax.rem(c + k, n_context)
            cp = pltpu.make_async_remote_copy(
                src_ref=tokens.at[pc, s], dst_ref=tok.at[s, c],
                send_sem=tok_s.at[s, k], recv_sem=tok_r.at[s, k],
                device_id={"context": pc}, device_id_type=MESH,
            )
            cp.start()
            outgoing.append(cp)
    own = []
    for s in range(seqs):
        cp = pltpu.make_async_copy(tokens.at[c, s], tok.at[s, c], own_s.at[s])
        cp.start()
        own.append(cp)

    def project(s, h):
        x = tok[s, h].astype(F32)
        y, _ = normalized(x)
        a = (y * gain[...]).astype(BF)
        qkv[s, pl.ds(pl.multiple_of(h * half, half), half), :] = dot(a, wqkv[...]).astype(BF)

    for s in range(seqs):
        own[s].wait()
        project(s, c)
    for cp in outgoing:
        cp.wait()
    crossing = []
    for k in range(1, n):
        j, pe, pc = peer(k)
        cp = pltpu.make_async_remote_copy(
            src_ref=cot.at[pc, :, pl.ds(pl.multiple_of(pe * slab, slab), slab), :],
            dst_ref=cot_m.at[pl.ds(e * seqs, seqs), c],
            send_sem=cot_s.at[k], recv_sem=cot_r.at[k],
            device_id={"expert": pe, "context": pc}, device_id_type=MESH,
        )
        cp.start()
        crossing.append(cp)
    local = pltpu.make_async_copy(
        cot.at[c, :, pl.ds(pl.multiple_of(e * slab, slab), slab), :],
        cot_m.at[pl.ds(e * seqs, seqs), c], own_s.at[seqs],
    )
    local.start()
    for k in range(1, n_context):
        for s in range(seqs):
            project(s, lax.rem(c + k, n_context))
    saves = [
        pltpu.make_async_copy(qkv, qkv_o, save_s.at[0]),
        pltpu.make_async_copy(tok, tok_a, save_s.at[1]),
    ]
    for cp in saves:
        cp.start()
    lane = lax.broadcasted_iota(jnp.int32, (qn, 128), 1)
    moving = []
    total = jnp.zeros((1, width), F32)
    for s in range(seqs):
        for qb in range(length // qn):
            kk = (qb + 1) * qn
            rows = pl.ds(qb * qn, qn)
            mask_bias(bias, kmark, qmark, s, qb * qn, qn)

            def pair(hp, _):
                at = pl.multiple_of(hp * 128, 128)
                q2 = qkv[s, rows, pl.ds(at, 128)] * BF(0.125)
                k2 = qkv[s, pl.ds(0, kk), pl.ds(width + at, 128)]
                v2 = qkv[s, pl.ds(0, kk), pl.ds(2 * width + at, 128)]
                outs = []
                for h in range(2):
                    mine = (lane >= 64) if h else (lane < 64)
                    qm = jnp.where(mine, q2, jnp.zeros_like(q2))
                    st = dot(k2, qm, ((1,), (1,))) + bias[pl.ds(0, kk), :]
                    top = jnp.max(st, 0, keepdims=True)
                    p = jnp.exp(st - top)
                    tot = jnp.sum(p, 0, keepdims=True)
                    lse_o[s, pl.ds(2 * hp + h, 1), rows] = top + jnp.log(tot)
                    low = (p * (1.0 / tot)).astype(BF)
                    outs.append(dot(low, v2, ((0,), (0,))))
                att[s, rows, pl.ds(at, 128)] = jnp.where(lane < 64, outs[0], outs[1]).astype(BF)
                return 0

            lax.fori_loop(0, width // 128, pair, 0)
            h = qb * qn // half
            attn_out = dot(att[s, rows, :], wout[...])
            within = qb * qn - h * half
            x = tok[s, h, pl.ds(within, qn), :].astype(F32)
            res[s, h, pl.ds(within, qn), :] = (x + attn_out).astype(BF)
            ok = kmark[s, rows, :] >= 0
            total += jnp.sum(jnp.where(ok, attn_out * attn_out, 0.0), 0, keepdims=True)
            if (qb + 1) * qn == (h + 1) * half:
                for k in range(1, n_expert):
                    pe = lax.rem(e + k, n_expert)
                    cp = pltpu.make_async_remote_copy(
                        src_ref=res.at[s, h, pl.ds(pl.multiple_of(pe * slab, slab), slab), :],
                        dst_ref=resid_m.at[e * seqs + s, h],
                        send_sem=res_s.at[s, h, k], recv_sem=res_r.at[s, h, k],
                        device_id={"expert": pe}, device_id_type=MESH,
                    )
                    cp.start()
                    moving.append(cp)
                cp = pltpu.make_async_copy(
                    res.at[s, h, pl.ds(pl.multiple_of(e * slab, slab), slab), :],
                    resid_m.at[e * seqs + s, h], res_s.at[s, h, 0],
                )
                cp.start()
                moving.append(cp)
    sq_o[...] = total
    keep = pltpu.make_async_copy(att, att_o, save_s.at[2])
    keep.start()
    for cp in saves + moving + crossing + [local, keep]:
        cp.wait()


def forward(tokens, cot, kmark, qmark, gain, wqkv, wout, n_expert, n_context):
    reps, seqs, half, width = tokens.shape
    length = half * n_context
    slab = half // n_expert
    group = seqs * n_expert
    n = n_expert * n_context
    sem = pltpu.SemaphoreType.DMA
    return pl.pallas_call(
        functools.partial(forward_kernel, n_expert=n_expert, n_context=n_context),
        out_shape=(
            jax.ShapeDtypeStruct((group, n_context, slab, width), BF),
            jax.ShapeDtypeStruct((group, n_context, slab, width), BF),
            jax.ShapeDtypeStruct((seqs, n_context, half, width), BF),
            jax.ShapeDtypeStruct((seqs, length, 3 * width), BF),
            jax.ShapeDtypeStruct((seqs, length, width), BF),
            jax.ShapeDtypeStruct((seqs, HEADS, length), F32),
            jax.ShapeDtypeStruct((1, width), F32),
        ),
        in_specs=[ANY, ANY, VM, VM, VM, VM, VM],
        out_specs=(ANY, ANY, ANY, ANY, ANY, VM, VM),
        scratch_shapes=[
            pltpu.VMEM((seqs, n_context, half, width), BF),
            pltpu.VMEM((seqs, length, 3 * width), BF),
            pltpu.VMEM((seqs, length, width), BF),
            pltpu.VMEM((seqs, n_context, half, width), BF),
            pltpu.VMEM((length, 256), F32),
            sem((seqs, n_context)), sem((seqs, n_context)),
            sem((n,)), sem((n,)),
            sem((seqs, n_context, n_expert)), sem((seqs, n_context, n_expert)),
            sem((seqs + 1,)), sem((3,)),
        ],
        compiler_params=pltpu.CompilerParams(
            collective_id=0, has_side_effects=True, vmem_limit_bytes=VMEM_LIMIT
        ),
        name="attend_forward",
    )(tokens, cot, kmark, qmark, gain, wqkv, wout)


def mix_phase(resid_low, cot, valid_m, gain_mix, w_control, w_in1, w_back1, n_expert, n_context):
    group, halves, slab, width = resid_low.shape
    n = n_expert * n_context
    rows = halves * slab
    resid = resid_low.reshape(group, rows, width).astype(F32)
    cot = cot.reshape(group, rows, width)
    here = valid_m.reshape(group, rows) > 0
    normed, norm_back = jax.vjp(lambda r, g: normalized(r)[0] * g, resid, gain_mix)
    u = normed.astype(BF)
    logits = jnp.einsum("spd,de->spe", u, w_control, preferred_element_type=F32)
    masked = jnp.where(here[..., None], logits, NEG_FILL)
    weights = jax.nn.softmax(masked, 0)
    low = weights.astype(BF)

    def to_owner(x):
        return lax.all_to_all(x, ("expert", "context"), 0, 0)

    mixed = to_owner(jnp.einsum("spe,spd->epd", low, u, preferred_element_type=F32).astype(BF))
    dexp = to_owner(jnp.einsum("spe,spd->epd", low, cot, preferred_element_type=F32).astype(BF))
    x = mixed.reshape(n * rows, width)
    de = dexp.reshape(n * rows, width)
    pre = dot(x, w_in1)
    act, gelu_back = jax.vjp(jax.nn.gelu, pre)
    act = act.astype(BF)
    eo = dot(act, w_back1).astype(BF)
    grad_back = dot(act, de, ((0,), (0,)))
    d_pre = gelu_back(dot(de, w_back1, ((1,), (1,))))[0].astype(BF)
    grad_in = dot(x, d_pre, ((0,), (0,)))
    dm = dot(d_pre, w_in1, ((1,), (1,))).astype(BF)
    eo = to_owner(eo.reshape(n, rows, width))
    dm = to_owner(dm.reshape(n, rows, width))
    mix_out = jnp.einsum("spe,epd->spd", low, eo, preferred_element_type=F32)
    out_full = resid + mix_out
    d_w = jnp.einsum("spd,epd->spe", cot, eo, preferred_element_type=F32) + jnp.einsum(
        "spd,epd->spe", u, dm, preferred_element_type=F32
    )
    d_logits = (weights * (d_w - jnp.sum(weights * d_w, 0))).astype(BF)
    grad_control = jnp.einsum("spd,spe->de", u, d_logits, preferred_element_type=F32)
    d_u = jnp.einsum("spe,de->spd", d_logits, w_control, preferred_element_type=F32) + jnp.einsum(
        "spe,epd->spd", low, dm, preferred_element_type=F32
    )
    d_norm, grad_gain_mix = norm_back(d_u)
    d_attn = (cot.astype(F32) + d_norm).astype(BF)
    okf = here.astype(F32)[..., None]
    sums = jnp.stack([jnp.sum(okf * out_full * out_full), jnp.sum(okf * mix_out * mix_out), jnp.sum(okf)])
    shape = (group, halves, slab, width)
    return d_attn.reshape(shape), out_full.astype(BF).reshape(shape), grad_in, grad_back, grad_control, grad_gain_mix, sums


def back_phase(d_attn, tok_a, qkv, att, lse, kmark, qmark, gain, wqkv, wout):
    seqs, length, width = d_attn.shape
    x = tok_a.astype(F32)
    normed, norm_back = jax.vjp(lambda r, g: normalized(r)[0] * g, x, gain)
    a = normed.astype(BF)
    grad_out = jnp.einsum("sld,sle->de", att, d_attn, preferred_element_type=F32)
    d_att = jnp.einsum("sle,de->sld", d_attn, wout, preferred_element_type=F32).astype(BF)

    def one(pack):
        qkv, d_att, lse, km, qm = pack
        q, k, v = (t.reshape(length, HEADS, -1) for t in jnp.split(qkv, 3, -1))
        do = d_att.reshape(length, HEADS, -1)
        i = jnp.arange(length)
        ok = (i[:, None] >= i[None, :]) & (km.T == qm.T)
        s = jnp.where(ok[None], jnp.einsum("qhd,khd->hqk", q, k, preferred_element_type=F32) * 0.125, NEG_FILL)
        p = jnp.exp(s - lse[..., None])
        dp = jnp.einsum("qhd,khd->hqk", do, v, preferred_element_type=F32)
        ds = (p * (dp - jnp.sum(p * dp, -1, keepdims=True))).astype(BF)
        dq = jnp.einsum("hqk,khd->qhd", ds, k, preferred_element_type=F32) * 0.125
        dk = jnp.einsum("hqk,qhd->khd", ds, q, preferred_element_type=F32) * 0.125
        dv = jnp.einsum("hqk,qhd->khd", p.astype(BF), do, preferred_element_type=F32)
        return jnp.concatenate([t.reshape(length, width) for t in (dq, dk, dv)], -1).astype(BF)

    d_qkv = lax.map(one, (qkv, d_att, lse, kmark, qmark))
    grad_qkv = jnp.einsum("sld,slc->dc", a, d_qkv, preferred_element_type=F32)
    d_a = jnp.einsum("slc,dc->sld", d_qkv, wqkv, preferred_element_type=F32)
    d_norm, grad_gain = norm_back(d_a)
    return (d_attn.astype(F32) + d_norm).astype(BF), grad_qkv, grad_out, grad_gain


def per_device(n_expert, n_context, tokens, gain_attn, wqkv, w_out, gain_mix, w_control, w_in, w_back, segments, valid, cotangent):
    reps, seqs, half, width = tokens.shape
    length = half * n_context
    slab = half // n_expert
    group = seqs * n_expert
    e, c = lax.axis_index("expert"), lax.axis_index("context")

    def pick(x, i, axis=0):
        return lax.dynamic_index_in_dim(x, i, axis, keepdims=False)

    seg_a, valid_a = pick(segments, c), pick(valid, c)
    kmark = jnp.where(valid_a > 0, seg_a, -1)[:, :, None]
    qmark = seg_a[:, None, :]
    valid_all = pick(lax.all_gather(valid, "expert"), c, 1).reshape(group, n_context, n_expert, slab)
    valid_m = pick(valid_all, e, 2)
    resid_m, cot_m, tok_a, qkv, att, lse, sq = forward(
        tokens, cotangent, kmark, qmark, gain_attn[None], wqkv, w_out, n_expert, n_context
    )
    d_attn_m, out_m, grad_in, grad_back, grad_control, grad_gain_mix, sums = mix_phase(
        resid_m, cot_m, valid_m, gain_mix, w_control, pick(w_in, c), pick(w_back, c), n_expert, n_context
    )
    d_attn = lax.all_to_all(d_attn_m, "expert", 0, 2, tiled=True).reshape(seqs, length, width)

    def home(x):
        x = x.reshape(n_expert, seqs, n_context, slab, width).transpose(0, 2, 1, 3, 4)
        x = x.reshape(n_expert * n_context, seqs, slab, width)
        x = lax.all_to_all(x, ("expert", "context"), 0, 0).reshape(n_expert, n_context, seqs, slab, width)
        return x.transpose(1, 2, 0, 3, 4).reshape(reps, seqs, half, width)

    output = home(out_m)
    d_tok, grad_qkv, grad_out, grad_gain = back_phase(
        d_attn, tok_a.reshape(seqs, length, width), qkv, att, lse, kmark, qmark, gain_attn, wqkv, w_out
    )
    d_tok = d_tok.reshape(seqs, n_context, half, width).transpose(1, 0, 2, 3)
    d_tokens = lax.all_to_all(d_tok, "context", 0, 0)

    def whole(g):
        g = lax.psum(g.astype(BF), "dp")
        return lax.all_gather(g, "context").astype(F32)

    squares = jnp.stack([sums[0], jnp.sum(sq), sums[1], sums[2]])
    grad_gain, grad_qkv, grad_out, grad_gain_mix, grad_control, squares = lax.psum(
        (grad_gain, grad_qkv, grad_out, grad_gain_mix, grad_control, squares), ("expert", "context", "dp")
    )
    stats = jnp.sqrt(squares[:3] / (squares[3] * width))
    return (
        output, d_tokens, grad_gain, grad_qkv, grad_out, grad_gain_mix, grad_control,
        whole(grad_in), whole(grad_back), stats,
    )


def solution(mesh):
    shards = P("dp", "expert", "context", None)
    rows = P("dp", "expert", None)
    experts = P("expert", None, None)
    return jax.shard_map(
        functools.partial(per_device, mesh.shape["expert"], mesh.shape["context"]),
        mesh=mesh,
        in_specs=(shards, P(), P(), P(), P(), P(), experts, experts, rows, rows, shards),
        out_specs=(shards, shards, P(), P(), P(), P(), P(), experts, experts, P()),
        check_vma=False,
    )
```

time: 1080 us -> 857 us (0.79)
  waiting for transfers between devices: 346 us -> 214 us
  local copies, waits for them, and re-layouts: 167 us -> 59.9 us
  Pallas kernels: 0 us -> 87.5 us
  matrix products: 351 us -> 270 us
  starting transfers between devices: 9.66 us -> 32.7 us
  other arithmetic: 121 us -> 105 us
    ppermute x2 -> x0, waiting for transfers between devices: 126 us -> none  [shifted(): return lax.ppermute(x, axis, pairs)]
    reduce_scatter x2 -> x0, waiting for transfers between devices: 107 us -> none  [the longest x1 55.3 us: per_device(): lax.psum_scatter(jnp.einsum('rspe,rspd->erpd', part_weights, u_low, prefe...]
    pallas_call x0 -> x1, Pallas kernels: none -> 87.5 us  [forward(): pl.pallas_call(functools.partial(forward_kernel, n_expert=n_expert, n_con...]
    dot_general x49 -> x29, matrix products: 351 us -> 270 us  [the longest x6 68.7 us: dot(): return lax.dot_general(a, b, (dims, ((), ())), preferred_element_type=F32)]
    psum x2, waiting for transfers between devices: 80 us -> 149 us  [the longest x1 98.2 us: whole(): g = lax.psum(g.astype(BF), 'dp')]
    all_to_all x0 -> x7, waiting for transfers between devices: none -> 65.6 us  [the longest x4 56.3 us: to_owner(): return lax.all_to_all(x, ('expert', 'context'), 0, 0)]
    unnamed x102 -> x61, local copies, waits for them, and re-layouts: 57.4 us -> 10.6 us
    slice x10 -> x1, local copies, waits for them, and re-layouts: 35.2 us -> 0.58 us  [per_device(): stats = jnp.sqrt(squares[:3] / (squares[3] * width))]
  transfers between devices with their start and end apart: 8 -> 11, of which waited for: 7 -> 7; matrix products, arithmetic and copies ran while one was open for 42% -> 44% of each run, Pallas kernels for 0% -> 0%
where the time goes in v1:
time: 857 us; the launch traced here: 852 us
  matrix products  270 us (32%)
  waiting for transfers between devices  214 us (25%)
  other arithmetic  105 us (12%)
  Pallas kernels  87.5 us (10%)
  blocking collectives  63.9 us (7%)
  local copies, waits for them, and re-layouts  59.9 us (7%)
  starting transfers between devices  32.7 us (4%)
  between operations  16.9 us (2%)
    psum x1, waiting for transfers between devices, whole(): g = lax.psum(g.astype(BF), 'dp')  98.2 us
    pallas_call x1, Pallas kernels, forward(): pl.pallas_call(functools.partial(forward_kernel, n_expert=n_expert, n_con...  87.5 us
    dot_general x6, matrix products, dot(): return lax.dot_general(a, b, (dims, ((), ())), preferred_element_type=F32)  68.7 us
    psum x1, blocking collectives, per_device(): lax.psum((grad_gain, grad_qkv, grad_out, grad_gain_mix, grad_control, squ...  57.5 us
    convert_element_type x2, other arithmetic, one(): ds = (p * (dp - jnp.sum(p * dp, -1, keepdims=True))).astype(BF)  56.8 us
    all_to_all x4, waiting for transfers between devices, to_owner(): return lax.all_to_all(x, ('expert', 'context'), 0, 0)  56.3 us
    psum x1, waiting for transfers between devices, per_device(): lax.psum((grad_gain, grad_qkv, grad_out, grad_gain_mix, grad_control, squ...  50.6 us
    dot_general x2, matrix products, one(): dp = jnp.einsum('qhd,khd->hqk', do, v, preferred_element_type=F32)  47.5 us
  transfers between devices with their start and end apart: 11, of which 7 were waited for; matrix products, arithmetic and copies ran while one was open for 44% of the time, Pallas kernels for 0%

profile of v1, /device:TPU:0, one launch (start us, length us, event | category | flops | bytes accessed | tf_op | source)
XLA Modules:
  0.0 851.6 jit_solution(4137238283563444510)
XLA Ops:
  8.0 6.5 all-gather
  16.7 87.5 %attend_forward.1 = (bf16[8,2,128,512]{3,2,1,0:T(8,128)(2,1)}, bf16[8,2,128,512]{3,2,1,0:T(8,128)(2,1)}, bf16[2,2,512,512]{3,2,1,0:T(8,128)(2,1)}, bf16[2,1024,1...) custom-call(bf16[2,2,512,512]{3,2,1,0:T(8,128)(2,1)} %tokens.1, ...), custom_call_target="tpu_custom_call" | custom-call | tf_op jit(solution)/shard_map/attend_forward/pallas_call | solution.py:196
  117.1 4.3 all-to-all-start
  126.4 21.5 %all-to-all-done = bf16[8,256,512]{2,1,0:T(8,128)(2,1)} async-done(((bf16[8,256,512]{2,1,0:T(8,128)(2,1)}), bf16[8,256,512]{2,1,0:T(8,128)(2,1)}, u32[]{:S(2)}, u32[]{:S(2)}) %all-to-all-start) | async-done | bytes 2097184 | tf_op jit(solution)/shard_map/all_to_all | solution.py:242
  147.9 4.9 all-to-all-start.3
  152.8 14.2 %multiply_convert_fusion.3 = (bf16[2048,2048]{1,0:T(8,128)(2,1)}, f32[2048,2048]{1,0:T(8,128)}) fusion(bf16[2048,512]{1,0:T(8,128)(2,1)} %bitcast.20, bf16[2,512,2048]{2,1,0:T(8,128)(2,1)} %param.19, s32[]{:T(128)S(6)} %select_n.37), kind=kOutput, calls=%fused_computation.28 | convolution fusion | flops 4332716032 | bytes 29360132 | tf_op jit(solution)/shard_map/dot_general | solution.py:20
  167.0 11.9 %all-to-all-done.3 = bf16[8,256,512]{2,1,0:T(8,128)(2,1)} async-done(((bf16[8,256,512]{2,1,0:T(8,128)(2,1)}), bf16[8,256,512]{2,1,0:T(8,128)(2,1)}, u32[]{:S(2)}, u32[]{:S(2)}) %all-to-all-start.3) | async-done | bytes 2097184 | tf_op jit(solution)/shard_map/all_to_all | solution.py:242
  179.0 10.0 %fusion.20 = bf16[1,2048,512]{2,1,0:T(8,128)(2,1)} fusion(bf16[2048,2048]{1,0:T(8,128)(2,1)} %get-tuple-element.137, bf16[2048,512]{1,0:T(8,128)(2,1)} %bitcast.32), kind=kOutput, calls=%fused_computation.55 | convolution fusion | flops 4296015872 | bytes 12582912 | tf_op jit(solution)/shard_map/dot_general | solution.py:20
  189.0 5.9 convolution_convert_fusion.3
  194.9 18.8 %fusion.16 = bf16[2048,2048]{1,0:T(8,128)(2,1)} fusion(f32[2048,2048]{1,0:T(8,128)} %get-tuple-element.138, bf16[2048,512]{1,0:T(8,128)(2,1)} %bitcast.32, bf16[2,2048,512]{2,1,0:T(8,128)(2,1)S(1)} %copy-done.23, s32[]{:T(128)S(6)} %select_n.37), kind=kOutput, calls=%fused_computation.27 | convolution fusion | flops 4378853376 | bytes 29360132 | tf_op jit(solution)/shard_map/dot_general | solution.py:20
  213.7 4.4 all-to-all-start.1
  218.1 9.9 %fusion.19 = bf16[1,512,2048]{2,1,0:T(8,128)(2,1)} fusion(bf16[2048,512]{1,0:T(8,128)(2,1)} %bitcast.20, bf16[2048,2048]{1,0:T(8,128)(2,1)} %fusion.16), kind=kOutput, calls=%fused_computation.54 | convolution fusion | flops 4296015872 | bytes 12582912 | tf_op jit(solution)/shard_map/dot_general | solution.py:20
  228.0 9.9 %convolution_convert_fusion.2 = bf16[2048,512]{1,0:T(8,128)(2,1)} fusion(bf16[2048,2048]{1,0:T(8,128)(2,1)} %fusion.16, bf16[2,512,2048]{2,1,0:T(8,128)(2,1)} %param.19, s32[]{:T(128)S(6)} %select_n.37), kind=kOutput, calls=%fused_computation.52 | convolution fusion | flops 4296015872 | bytes 12582916 | tf_op jit(solution)/shard_map/dot_general | solution.py:20
  237.9 6.3 all-to-all-done.1
  244.2 4.3 all-to-all-start.4
  251.1 5.5 fusion.31
  258.2 16.5 %all-to-all-done.4 = bf16[8,256,512]{2,1,0:T(8,128)(2,1)} async-done(((bf16[8,256,512]{2,1,0:T(8,128)(2,1)}), bf16[8,256,512]{2,1,0:T(8,128)(2,1)}, u32[]{:S(2)}, u32[]{:S(2)}) %all-to-all-start.4) | async-done | bytes 2097184 | tf_op jit(solution)/shard_map/all_to_all | solution.py:242
  274.7 5.6 fusion.28
  281.9 5.0 fusion.26
  286.9 98.2 %all-reduce.8.cloned.1.call-done = (bf16[1,512,2048]{2,1,0:T(8,128)(2,1)}, bf16[1,2048,512]{2,1,0:T(8,128)(2,1)}) async-done(((bf16[1,512,2048]{2,1,0:T(8,128)(2,1)}, bf16[1,2048,512]{2,1,0:T(8,128)(2,1)}), (bf16[1,512,2048]{2,1,0:T(8,128)(2,1)}, bf16[1,2048,512]{2,1,0:T(8,128)(2,1)})) %all-reduce.8.cloned.1.call-update) | async-done | bytes 4194320 | tf_op jit(solution)/shard_map/psum | solution.py:343
  385.2 5.5 multiply_reduce_fusion.5
  396.3 5.0 all-to-all-start.5
  405.8 7.2 fusion.17
  417.7 9.3 %all-to-all-done.5 = bf16[8,2,128,512]{3,2,1,0:T(8,128)(2,1)} async-done(((bf16[8,2,128,512]{3,2,1,0:T(8,128)(2,1)}), bf16[8,2,128,512]{3,2,1,0:T(8,128)(2,1)}, u32[]{:S(2)}, u32[]{:S(2)}) %all-to-all-start.5) | async-done | bytes 2097184 | tf_op jit(solution)/shard_map/all_to_all | solution.py:327
  427.0 4.5 all-to-all-start.2
  437.4 239.7 %while.10 = (s32[]{:T(128)}, bf16[2,1024,1536]{1,2,0:T(8,128)(2,1)}, bf16[2,1024,1536]{2,1,0:T(8,128)(2,1)}, s32[2,1024,1]{1,0,2:T(2,128)S(1)}, s32[2,1,1024]{2,...) while((s32[]{:T(128)}, bf16[2,1024,1536]{1,2,0:T(8,128)(2,1)}, ...), condition=%wide.region_9.10_spmd, body=%wide.region_7.9_spmd.sunk | while | flops 5509734400 | bytes 295952480 | solution.py:299
  440.8 3.8 constant_dynamic-slice_fusion.10
  444.6 4.6 copy.201
  452.4 15.1 %fusion.127 = f32[8,1024,1024]{1,2,0:T(8,128)} fusion(bf16[1024,8,64]{0,2,1:T(8,128)(2,1)S(1)} %bitcast.240, bf16[1024,8,64]{0,2,1:T(8,128)(2,1)S(1)} %bitcast.242), kind=kOutput, calls=%fused_computation.135.clone.1 | convolution fusion | flops 1073741824 | bytes 35651584 | tf_op jit(solution)/shard_map/while/body/eval_jaxpr/qhd,khd->hqk/dot_general | solution.py:290
  467.5 15.9 %fusion.129 = bf16[8,64,1024]{2,1,0:T(8,128)(2,1)} fusion(bf16[1024,8,64]{0,2,1:T(8,128)(2,1)} %bitcast.245, f32[8,1024,1024]{1,2,0:T(8,128)} %fusion.127, f32[8,1024]{1,0:T(8,128)S(1)} %dynamic-slice_bitcast_fusion.3, pred[1024,1024]{0,1:T(8,128)(4,1)S(1)} %fusion.128), kind=kOutput, calls=%fused_computation.11.clone.1 | convolution fusion | flops 1107820544 | bytes 36732928 | tf_op jit(solution)/shard_map/while/body/eval_jaxpr/hqk,qhd->khd/dot_general | solution.py:296
  483.3 23.7 %multiply_reduce_fusion.8 = (f32[8,1024]{1,0:T(8,128)S(1)}, f32[8,1024,1024]{1,2,0:T(8,128)}) fusion(f32[8,1024,1024]{1,2,0:T(8,128)} %fusion.127, f32[8,1024]{1,0:T(8,128)S(1)} %dynamic-slice_bitcast_fusion.3, pred[1024,1024]{0,1:T(8,128)(4,1)S(1)} %fusion.128, bf16[1024,8,64]{0,2,1:T(8,128)(2,1)} %bitcast.246, bf16[1024,8,64]{0,2,1:T(8,128)(2,1)} %bitcast.247), kind=kOutput, calls=%fused_computation.1.clone.1 | convolution fusion | flops 1115676672 | bytes 70320128 | tf_op jit(solution)/shard_map/while/body/eval_jaxpr/qhd,khd->hqk/dot_general | solution.py:292
  507.1 28.4 %multiply_convert_fusion.9 = bf16[8,1024,1024]{1,2,0:T(8,128)(2,1)} fusion(f32[8,1024,1024]{1,2,0:T(8,128)} %get-tuple-element.194, f32[8,1024,1024]{1,2,0:T(8,128)} %fusion.127, f32[8,1024]{1,0:T(8,128)S(1)} %get-tuple-element.195, f32[8,1024]{1,0:T(8,128)S(1)} %dynamic-slice_bitcast_fusion.3, pred[1024,1024]{0,1:T(8,128)(4,1)S(1)} %fusion.128), kind=kLoop, calls=%fused_computation.clone.1 | loop fusion | flops 50331648 | bytes 85000192 | tf_op jit(solution)/shard_map/while/body/eval_jaxpr/convert_element_type | solution.py:293
  535.5 8.9 %multiply_convert_fusion.11 = bf16[8,64,1024]{2,1,0:T(8,128)(2,1)S(1)} fusion(bf16[1024,8,64]{0,2,1:T(8,128)(2,1)S(1)} %bitcast.243, bf16[8,1024,1024]{1,2,0:T(8,128)(2,1)} %multiply_convert_fusion.9), kind=kOutput, calls=%fused_computation.10.clone.1 | convolution fusion | flops 1074790400 | bytes 18874368 | tf_op jit(solution)/shard_map/while/body/eval_jaxpr/hqk,khd->qhd/dot_general | solution.py:294
  544.4 11.0 %multiply_convert_fusion.10 = bf16[8,64,1024]{2,1,0:T(8,128)(2,1)S(1)} fusion(bf16[1024,8,64]{0,2,1:T(8,128)(2,1)S(1)} %bitcast.241, bf16[8,1024,1024]{1,2,0:T(8,128)(2,1)} %multiply_convert_fusion.9), kind=kOutput, calls=%fused_computation.9.clone.1 | convolution fusion | flops 1074790400 | bytes 18874368 | tf_op jit(solution)/shard_map/while/body/eval_jaxpr/hqk,qhd->khd/dot_general | solution.py:295
  565.3 4.6 copy.201
  573.0 13.1 %fusion.127 = f32[8,1024,1024]{1,2,0:T(8,128)} fusion(bf16[1024,8,64]{0,2,1:T(8,128)(2,1)S(1)} %bitcast.240, bf16[1024,8,64]{0,2,1:T(8,128)(2,1)S(1)} %bitcast.242), kind=kOutput, calls=%fused_computation.135.clone.1 | convolution fusion | flops 1073741824 | bytes 35651584 | tf_op jit(solution)/shard_map/while/body/eval_jaxpr/qhd,khd->hqk/dot_general | solution.py:290
  586.1 15.9 %fusion.129 = bf16[8,64,1024]{2,1,0:T(8,128)(2,1)} fusion(bf16[1024,8,64]{0,2,1:T(8,128)(2,1)} %bitcast.245, f32[8,1024,1024]{1,2,0:T(8,128)} %fusion.127, f32[8,1024]{1,0:T(8,128)S(1)} %dynamic-slice_bitcast_fusion.3, pred[1024,1024]{0,1:T(8,128)(4,1)S(1)} %fusion.128), kind=kOutput, calls=%fused_computation.11.clone.1 | convolution fusion | flops 1107820544 | bytes 36732928 | tf_op jit(solution)/shard_map/while/body/eval_jaxpr/hqk,qhd->khd/dot_general | solution.py:296
  602.0 23.7 %multiply_reduce_fusion.8 = (f32[8,1024]{1,0:T(8,128)S(1)}, f32[8,1024,1024]{1,2,0:T(8,128)}) fusion(f32[8,1024,1024]{1,2,0:T(8,128)} %fusion.127, f32[8,1024]{1,0:T(8,128)S(1)} %dynamic-slice_bitcast_fusion.3, pred[1024,1024]{0,1:T(8,128)(4,1)S(1)} %fusion.128, bf16[1024,8,64]{0,2,1:T(8,128)(2,1)} %bitcast.246, bf16[1024,8,64]{0,2,1:T(8,128)(2,1)} %bitcast.247), kind=kOutput, calls=%fused_computation.1.clone.1 | convolution fusion | flops 1115676672 | bytes 70320128 | tf_op jit(solution)/shard_map/while/body/eval_jaxpr/qhd,khd->hqk/dot_general | solution.py:292
  625.8 28.4 %multiply_convert_fusion.9 = bf16[8,1024,1024]{1,2,0:T(8,128)(2,1)} fusion(f32[8,1024,1024]{1,2,0:T(8,128)} %get-tuple-element.194, f32[8,1024,1024]{1,2,0:T(8,128)} %fusion.127, f32[8,1024]{1,0:T(8,128)S(1)} %get-tuple-element.195, f32[8,1024]{1,0:T(8,128)S(1)} %dynamic-slice_bitcast_fusion.3, pred[1024,1024]{0,1:T(8,128)(4,1)S(1)} %fusion.128), kind=kLoop, calls=%fused_computation.clone.1 | loop fusion | flops 50331648 | bytes 85000192 | tf_op jit(solution)/shard_map/while/body/eval_jaxpr/convert_element_type | solution.py:293
  654.2 8.9 %multiply_convert_fusion.11 = bf16[8,64,1024]{2,1,0:T(8,128)(2,1)S(1)} fusion(bf16[1024,8,64]{0,2,1:T(8,128)(2,1)S(1)} %bitcast.243, bf16[8,1024,1024]{1,2,0:T(8,128)(2,1)} %multiply_convert_fusion.9), kind=kOutput, calls=%fused_computation.10.clone.1 | convolution fusion | flops 1074790400 | bytes 18874368 | tf_op jit(solution)/shard_map/while/body/eval_jaxpr/hqk,khd->qhd/dot_general | solution.py:294
  663.1 11.0 %multiply_convert_fusion.10 = bf16[8,64,1024]{2,1,0:T(8,128)(2,1)S(1)} fusion(bf16[1024,8,64]{0,2,1:T(8,128)(2,1)S(1)} %bitcast.241, bf16[8,1024,1024]{1,2,0:T(8,128)(2,1)} %multiply_convert_fusion.9), kind=kOutput, calls=%fused_computation.9.clone.1 | convolution fusion | flops 1074790400 | bytes 18874368 | tf_op jit(solution)/shard_map/while/body/eval_jaxpr/hqk,qhd->khd/dot_general | solution.py:295
  677.2 8.8 %multiply_reduce_fusion.3 = (f32[2,1024]{1,0:T(2,128)S(1)}, f32[2,1024,512]{2,1,0:T(8,128)S(1)}) fusion(bf16[2,2,512,512]{3,2,1,0:T(8,128)(2,1)} %get-tuple-element.59, f32[2,1024]{1,0:T(2,128)S(1)} %bitcast.268, f32[512]{0:T(512)S(1)} %copy-done.20, bf16[2,1024,1536]{1,2,0:T(8,128)(2,1)} %get-tuple-element.58, bf16[512,1536]{1,0:T(8,128)(2,1)} %wqkv.1), kind=kOutput, calls=%fused_computation.42 | convolution fusion | flops 3226466304 | bytes 14174208 | tf_op jit(solution)/shard_map/slc,dc->sld/dot_general | solution.py:301
  691.4 5.1 convolution_bitcast_fusion
  701.8 4.9 all-to-all-start.6
  711.7 57.5 %all-reduce = (f32[512]{0:T(512)}, f32[512]{0:T(512)}, f32[512,8]{0,1:T(8,128)}, f32[4]{0:T(128)S(1)}) all-reduce(f32[512]{0:T(512)S(1)} %get-tuple-element.92, f32[512]{0:T(512)S(1)} %copy-done.21, f32[512,8]{0,1:T(8,128)S(1)} %convolution_bitcast_fusion.2, ...), channel_id=1, replica_groups=mesh['expert'=4,'context'=2,'dp'=4] {'expert','context','dp'}, use_global_device_ids=true, to_apply=%region_15.16 | all-reduce | flops 5124 | bytes 40992 | tf_op jit(solution)/shard_map/psum | solution.py:347
  774.1 6.8 convert_element_type.137
  780.9 6.7 convert_element_type.135
  787.6 50.6 %all-reduce.6.cloned.1.call-done = (f32[512,1536]{1,0:T(8,128)}, f32[512,512]{1,0:T(8,128)}) async-done(((f32[512,1536]{1,0:T(8,128)}, f32[512,512]{1,0:T(8,128)}), (f32[512,1536]{1,0:T(8,128)}, f32[512,512]{1,0:T(8,128)})) %all-reduce.6.cloned.1.call-update) | async-done | bytes 4194320 | tf_op jit(solution)/shard_map/psum | solution.py:347
  (144 shorter events, 94.2 us)
Async XLA Ops:
  8.0 103.0 %copy-start = (bf16[512,8]{0,1:T(8,128)(2,1)S(1)}, bf16[512,8]{0,1:T(8,128)(2,1)}, u32[]{:S(2)}) copy-start(bf16[512,8]{0,1:T(8,128)(2,1)} %param.18) | copy-start | bytes 24580
  15.3 1.4 copy-start.16
  16.7 92.1 %copy-start.19 = (f32[512]{0:T(512)S(1)}, f32[512]{0:T(512)}, u32[]{:S(2)}) copy-start(f32[512]{0:T(512)} %param.17) | copy-start | bytes 6148
  104.2 4.6 copy-start.2
  109.7 1.3 copy-start.3
  117.1 30.9 %all-to-all-start = ((bf16[8,256,512]{2,1,0:T(8,128)(2,1)}), bf16[8,256,512]{2,1,0:T(8,128)(2,1)}, u32[]{:S(2)}, u32[]{:S(2)}) async-start(bf16[8,256,512]{2,1,0:T(8,128)(2,1)} %copy.120), calls=%async_computation | async-start | bytes 4194304 | tf_op jit(solution)/shard_map/all_to_all | solution.py:242
  147.9 31.0 %all-to-all-start.3 = ((bf16[8,256,512]{2,1,0:T(8,128)(2,1)}), bf16[8,256,512]{2,1,0:T(8,128)(2,1)}, u32[]{:S(2)}, u32[]{:S(2)}) async-start(bf16[8,256,512]{2,1,0:T(8,128)(2,1)} %copy.130), calls=%async_computation.3 | async-start | bytes 4194304 | tf_op jit(solution)/shard_map/all_to_all | solution.py:242
  179.0 10.0 %copy-start.23 = (bf16[2,2048,512]{2,1,0:T(8,128)(2,1)S(1)}, bf16[2,2048,512]{2,1,0:T(8,128)(2,1)}, u32[]{:S(2)}) copy-start(bf16[2,2048,512]{2,1,0:T(8,128)(2,1)} %param.20) | copy-start | bytes 12582916
  179.0 10.0 %copy-start.24 = (bf16[2048,2048]{1,0:T(8,128)(2,1)S(1)}, bf16[2048,2048]{1,0:T(8,128)(2,1)}, u32[]{:S(2)}) copy-start(bf16[2048,2048]{1,0:T(8,128)(2,1)} %get-tuple-element.137) | copy-start | bytes 25165828
  213.7 30.6 %all-to-all-start.1 = ((bf16[8,256,512]{2,1,0:T(8,128)(2,1)}), bf16[8,256,512]{2,1,0:T(8,128)(2,1)}, u32[]{:S(2)}, u32[]{:S(2)}) async-start(bf16[8,256,512]{2,1,0:T(8,128)(2,1)} %bitcast.259), calls=%async_computation.1 | async-start | bytes 4194304 | tf_op jit(solution)/shard_map/all_to_all | solution.py:242
  218.0 167.1 %all-reduce.8.cloned.1.call-start = ((), (), s32[]{:S(2)}) async-start(), calls=%async_computation.10 | async-start | bytes 8388608 | tf_op jit(solution)/shard_map/psum | solution.py:343
  244.2 30.5 %all-to-all-start.4 = ((bf16[8,256,512]{2,1,0:T(8,128)(2,1)}), bf16[8,256,512]{2,1,0:T(8,128)(2,1)}, u32[]{:S(2)}, u32[]{:S(2)}) async-start(bf16[8,256,512]{2,1,0:T(8,128)(2,1)} %bitcast.260), calls=%async_computation.4 | async-start | bytes 4194304 | tf_op jit(solution)/shard_map/all_to_all | solution.py:242
  248.6 525.5 %all-gather.6.cloned.1.call-start = ((), (), s32[]{:S(2)}) async-start(), calls=%async_computation.8 | async-start | bytes 6291456 | tf_op jit(solution)/shard_map/all_gather | solution.py:344
  385.2 5.6 copy-start.14
  390.7 2.7 copy-start.9
  396.3 30.7 %all-to-all-start.5 = ((bf16[8,2,128,512]{3,2,1,0:T(8,128)(2,1)}), bf16[8,2,128,512]{3,2,1,0:T(8,128)(2,1)}, u32[]{:S(2)}, u32[]{:S(2)}) async-start(bf16[8,2,128,512]{3,2,1,0:T(8,128)(2,1)} %bitcast.256), calls=%async_computation.5 | async-start | bytes 4194304 | tf_op jit(solution)/shard_map/all_to_all | solution.py:327
  427.0 7.7 copy-start.13
  427.0 274.8 %all-to-all-start.2 = ((bf16[8,2,128,512]{3,2,1,0:T(8,128)(2,1)}), bf16[8,2,128,512]{3,2,1,0:T(8,128)(2,1)}, u32[]{:S(2)}, u32[]{:S(2)}) async-start(bf16[8,2,128,512]{3,2,1,0:T(8,128)(2,1)} %bitcast.26), calls=%async_computation.2 | async-start | bytes 4194304 | tf_op jit(solution)/shard_map/all_to_all | solution.py:332
  431.5 349.4 %all-gather.4.cloned.1.call-start = ((), (), s32[]{:S(2)}) async-start(), calls=%async_computation.7 | async-start | bytes 6291456 | tf_op jit(solution)/shard_map/all_gather | solution.py:344
  433.3 1.4 copy-start.6
  437.3 400.8 %all-reduce.6.cloned.1.call-start = ((), (), s32[]{:S(2)}) async-start(), calls=%async_computation.9 | async-start | bytes 8388608 | tf_op jit(solution)/shard_map/psum | solution.py:347
  437.4 239.8 %copy-start.17 = (f32[1,2,2,512]{3,1,2,0:T(2,128)S(1)}, f32[1,2,2,512]{3,1,2,0:T(2,128)}, u32[]{:S(2)}) copy-start(f32[1,2,2,512]{3,1,2,0:T(2,128)} %copy.163) | copy-start | bytes 24580
  437.4 239.8 %copy-start.20 = (f32[512]{0:T(512)S(1)}, f32[512]{0:T(512)}, u32[]{:S(2)}) copy-start(f32[512]{0:T(512)} %param.14) | copy-start | bytes 6148
  677.1 8.8 %copy-start.18 = (f32[1,2,2,512]{3,1,2,0:T(2,128)S(1)}, f32[1,2,2,512]{3,1,2,0:T(2,128)}, u32[]{:S(2)}) copy-start(f32[1,2,2,512]{3,1,2,0:T(2,128)} %copy.162) | copy-start | bytes 24580
  677.2 8.9 %copy-start.7 = (bf16[4,2,2,128,512]{4,3,0,2,1:T(8,128)(2,1)S(1)}, bf16[4,2,2,128,512]{4,3,0,2,1:T(8,128)(2,1)}, u32[]{:S(2)}) copy-start(bf16[4,2,2,128,512]{4,3,0,2,1:T(8,128)(2,1)} %copy-done.6) | copy-start | bytes 6291460
  677.2 8.9 %copy-start.11 = (bf16[2,1024,512]{2,1,0:T(8,128)(2,1)S(1)}, bf16[2,1024,512]{2,1,0:T(8,128)(2,1)}, u32[]{:S(2)}) copy-start(bf16[2,1024,512]{2,1,0:T(8,128)(2,1)} %get-tuple-element.60) | copy-start | bytes 6291460
  686.0 5.4 copy-start.8
  686.0 3.1 copy-start.5
  686.0 5.4 slice-start
  689.1 2.3 slice-start.1
  700.3 6.5 copy-start.22
  700.3 11.1 %copy-start.4 = (bf16[8,256,512]{2,1,0:T(8,128)(2,1)S(1)}, bf16[8,256,512]{2,1,0:T(8,128)(2,1)}, u32[]{:S(2)}) copy-start(bf16[8,256,512]{2,1,0:T(8,128)(2,1)} %copy-done.3) | copy-start | bytes 6291460
  700.3 11.1 %copy-start.15 = (bf16[8,256,8]{1,2,0:T(8,128)(2,1)S(1)}, bf16[8,256,8]{1,2,0:T(8,128)(2,1)}, u32[]{:S(2)}) copy-start(bf16[8,256,8]{1,2,0:T(8,128)(2,1)} %copy-done.14) | copy-start | bytes 98308
  701.8 10.0 %copy-start.21 = (f32[512]{0:T(512)S(1)}, f32[512]{0:T(512)}, u32[]{:S(2)}) copy-start(f32[512]{0:T(512)} %get-tuple-element.90) | copy-start | bytes 6148
  701.8 72.3 %all-to-all-start.6 = ((bf16[2,2,512,512]{3,2,1,0:T(8,128)(2,1)}), bf16[2,2,512,512]{3,2,1,0:T(8,128)(2,1)}, u32[]{:S(2)}, u32[]{:S(2)}) async-start(bf16[2,2,512,512]{3,2,1,0:T(8,128)(2,1)} %bitcast.253), calls=%async_computation.6 | async-start | bytes 4194304 | tf_op jit(solution)/shard_map/all_to_all | solution.py:340
  838.2 3.2 copy-start.10
  838.2 4.9 copy-start.12
  838.2 5.8 copy-start.1
Sparse Core Ops, SparseCore 0:
  228.1 156.9 all-reduce.7
  386.7 63.4 all-gather.5
  451.9 59.0 all-gather.3
Sparse Core Ops, SparseCore 1:
  696.7 141.4 all-reduce.5

commit v2 on v1

--- a/solution.py
+++ b/solution.py
@@ -224,83 +224,387 @@
     )(tokens, cot, kmark, qmark, gain, wqkv, wout)
 
 
-def mix_phase(resid_low, cot, valid_m, gain_mix, w_control, w_in1, w_back1, n_expert, n_context):
-    group, halves, slab, width = resid_low.shape
+def mix_kernel(
+    resid_m, cot_m, ok_m, gain, wc, w_in, w_back,
+    d_attn, out_m, gi_o, gb_o, gc_o, gm_o, sq_o,
+    res, cot, u, wts, big, mixed, dexp, xs, des, eos, dms, eor, dmr, win, wback, gi, gbt, dat, out, glow,
+    go_s, go_r, back_s, back_r, at_s, at_r, in_s, save_s,
+    *, n_expert, n_context,
+):
+    e, c, me, n, peer = ring(n_expert, n_context)
+    group, halves, slab, width = res.shape
+    seqs = group // n_expert
+    ff = win.shape[1]
+    experts = n
+    span = max(16, 256 // group)
+    steps = slab // span
+    chunk = 512 // slab
+    loads = [
+        pltpu.make_async_copy(resid_m, res, in_s.at[0]),
+        pltpu.make_async_copy(cot_m, cot, in_s.at[1]),
+        pltpu.make_async_copy(w_in.at[c], win, in_s.at[2]),
+        pltpu.make_async_copy(w_back.at[c], wback, in_s.at[3]),
+    ]
+    for cp in loads:
+        cp.start()
+    enter(peer, n)
+    rows, cols = group * span, experts * span
+    spread = (
+        lax.broadcasted_iota(jnp.int32, (experts, cols), 1) // span
+        == lax.broadcasted_iota(jnp.int32, (experts, cols), 0)
+    ).astype(BF)
+    gather = (
+        lax.broadcasted_iota(jnp.int32, (cols, experts), 0) // span
+        == lax.broadcasted_iota(jnp.int32, (cols, experts), 1)
+    ).astype(BF)
+    diag = lax.rem(lax.broadcasted_iota(jnp.int32, (rows, cols), 0), span) == lax.rem(
+        lax.broadcasted_iota(jnp.int32, (rows, cols), 1), span
+    )
+    loads[0].wait()
+    loads[1].wait()
+    sent = []
+    for h in range(halves):
+
+        def first(g, _):
+            at = pl.ds(pl.multiple_of(g * span, span), span)
+            r = res[:, h, at, :].reshape(rows, width).astype(F32)
+            normed, _ = normalized(r)
+            ug = (normed * gain[...]).astype(BF)
+            u[:, h, at, :] = ug.reshape(group, span, width)
+            ok = ok_m[:, h, at, :].reshape(rows, 1)
+            logits = jnp.where(ok > 0, dot(ug, wc[...]), NEG_FILL).reshape(group, span, experts)
+            ex = jnp.exp(logits - jnp.max(logits, 0, keepdims=True))
+            w = (ex / jnp.sum(ex, 0, keepdims=True)).reshape(rows, experts)
+            wts[h * steps + g] = w
+            wide = jnp.where(diag, dot(w.astype(BF), spread), 0.0).astype(BF)
+            big[h * steps + g] = wide
+            cg = cot[:, h, at, :].reshape(rows, width)
+            mixed[h, :, at, :] = dot(wide, ug, ((0,), (0,))).astype(BF).reshape(experts, span, width)
+            dexp[h, :, at, :] = dot(wide, cg, ((0,), (0,))).astype(BF).reshape(experts, span, width)
+            return 0
+
+        lax.fori_loop(0, steps, first, 0)
+        for i, (src, dst) in enumerate(((mixed, xs), (dexp, des))):
+            dst[h, 0] = src[h, me]
+            for k in range(1, n):
+                j, pe, pc = peer(k)
+                cp = pltpu.make_async_remote_copy(
+                    src_ref=src.at[h, j], dst_ref=dst.at[h, k],
+                    send_sem=go_s.at[i, h, k], recv_sem=go_r.at[i, h, k],
+                    device_id={"expert": pe, "context": pc}, device_id_type=MESH,
+                )
+                cp.start()
+                sent.append((i, h, k, cp))
+    loads[2].wait()
+    loads[3].wait()
+    tile = 512
+    gi[...] = jnp.zeros_like(gi)
+    gbt[...] = jnp.zeros_like(gbt)
+    returned = []
+    for h in range(halves):
+        for kg in range(n // chunk):
+            slots = range(kg * chunk, (kg + 1) * chunk)
+            for i, hh, k, cp in sent:
+                if hh == h and k in slots:
+                    cp.wait_recv()
+            x = xs[h, pl.ds(kg * chunk, chunk)].reshape(chunk * slab, width)
+            de = des[h, pl.ds(kg * chunk, chunk)].reshape(chunk * slab, width)
+            xt, det = x.T, de.T
+
+            def expert_tile(f, carry):
+                eo, dm = carry
+                at = pl.ds(pl.multiple_of(f * tile, tile), tile)
+                pre = dot(x, win[:, at])
+                sq = pre * pre
+                t = jnp.tanh(0.7978845608028654 * pre * (1.0 + 0.044715 * sq))
+                act = (0.5 * pre * (1.0 + t)).astype(BF)
+                slope = 0.5 * (1.0 + t) + 0.5 * pre * (1.0 - t * t) * (
+                    0.7978845608028654 * (1.0 + 3 * 0.044715 * sq)
+                )
+                d_pre = (slope * dot(de, wback[at, :], ((1,), (1,)))).astype(BF)
+                gbt[:, at] += dot(det, act)
+                gi[:, at] += dot(xt, d_pre)
+                return eo + dot(act, wback[at, :]), dm + dot(d_pre, win[:, at], ((1,), (1,)))
+
+            zero = jnp.zeros((chunk * slab, width), F32)
+            eo, dm = lax.fori_loop(0, ff // tile, expert_tile, (zero, zero))
+            eos[h, pl.ds(kg * chunk, chunk)] = eo.astype(BF).reshape(chunk, slab, width)
+            dms[h, pl.ds(kg * chunk, chunk)] = dm.astype(BF).reshape(chunk, slab, width)
+            for i, (src, dst) in enumerate(((eos, eor), (dms, dmr))):
+                for k in slots:
+                    if k == 0:
+                        dst[h, me] = src[h, 0]
+                        continue
+                    j, pe, pc = peer(n - k)
+                    cp = pltpu.make_async_remote_copy(
+                        src_ref=src.at[h, k], dst_ref=dst.at[h, me],
+                        send_sem=back_s.at[i, h, k], recv_sem=back_r.at[i, h, k],
+                        device_id={"expert": pe, "context": pc}, device_id_type=MESH,
+                    )
+                    cp.start()
+                    returned.append((i, h, k, cp))
+    glow[0] = gi[...].astype(BF)
+    keep = [pltpu.make_async_copy(glow.at[0], gi_o, save_s.at[0])]
+    keep[0].start()
+    for f in range(ff // tile):
+        glow[1, :, pl.ds(f * tile, tile)] = gbt[:, pl.ds(f * tile, tile)].astype(BF)
+    keep.append(pltpu.make_async_copy(glow.at[1], gb_o, save_s.at[1]))
+    keep[1].start()
+    gc_o[...] = jnp.zeros_like(gc_o)
+    gm_o[...] = jnp.zeros_like(gm_o)
+    sq_o[...] = jnp.zeros_like(sq_o)
+    moving = []
+    for h in range(halves):
+        for i, hh, k, cp in returned:
+            if hh == h:
+                cp.wait_recv()
+
+        def second(g, _):
+            at = pl.ds(pl.multiple_of(g * span, span), span)
+            r = res[:, h, at, :].reshape(rows, width).astype(F32)
+            normed, rstd = normalized(r)
+            ug = u[:, h, at, :].reshape(rows, width)
+            cg = cot[:, h, at, :].reshape(rows, width)
+            ok = ok_m[:, h, at, :].reshape(rows, 1) > 0
+            eg = eor[h, :, at, :].reshape(cols, width)
+            dg = dmr[h, :, at, :].reshape(cols, width)
+            wide = big[h * steps + g]
+            w = wts[h * steps + g]
+            mix = dot(wide, eg)
+            full = r + mix
+            out[:, h, at, :] = full.astype(BF).reshape(group, span, width)
+            sq_o[pl.ds(0, 1), :] += jnp.sum(jnp.where(ok, full * full, 0.0), 0, keepdims=True)
+            sq_o[pl.ds(1, 1), :] += jnp.sum(jnp.where(ok, mix * mix, 0.0), 0, keepdims=True)
+            dw = jnp.where(diag, dot(cg, eg, ((1,), (1,))) + dot(ug, dg, ((1,), (1,))), 0.0)
+            high = dw.astype(BF)
+            rest = (dw - high.astype(F32)).astype(BF)
+            dw = dot(high, gather) + dot(rest, gather)
+            inner = jnp.sum((w * dw).reshape(group, span, experts), 0, keepdims=True)
+            d_log = (
+                (w.reshape(group, span, experts) * (dw.reshape(group, span, experts) - inner))
+                .reshape(rows, experts)
+                .astype(BF)
+            )
+            gc_o[...] += dot(ug, d_log, ((0,), (0,)))
+            d_u = dot(d_log, wc[...], ((1,), (1,))) + dot(wide, dg)
+            gm_o[...] += jnp.sum(d_u * normed, 0, keepdims=True)
+            q = d_u * gain[...]
+            d_res = cg.astype(F32) + rstd * (
+                q - jnp.mean(q, -1, keepdims=True) - normed * jnp.mean(q * normed, -1, keepdims=True)
+            )
+            dat[:, h, at, :] = d_res.astype(BF).reshape(group, span, width)
+            return 0
+
+        lax.fori_loop(0, steps, second, 0)
+        mine = pl.ds(pl.multiple_of(e * slab, slab), slab)
+        for k in range(1, n_expert):
+            pe = lax.rem(e + k, n_expert)
+            cp = pltpu.make_async_remote_copy(
+                src_ref=dat.at[pl.ds(pe * seqs, seqs), h], dst_ref=d_attn.at[:, h, mine, :],
+                send_sem=at_s.at[h, k], recv_sem=at_r.at[h, k],
+                device_id={"expert": pe}, device_id_type=MESH,
+            )
+            cp.start()
+            moving.append(cp)
+        cp = pltpu.make_async_copy(
+            dat.at[pl.ds(e * seqs, seqs), h], d_attn.at[:, h, mine, :], at_s.at[h, 0]
+        )
+        cp.start()
+        moving.append(cp)
+    cp = pltpu.make_async_copy(out, out_m, save_s.at[2])
+    cp.start()
+    for _, _, _, sending in sent + returned:
+        sending.wait_send()
+    for cp in moving + keep + [cp]:
+        cp.wait()
+
+
+def mix(resid_m, cot_m, ok_m, gain, wc, w_in, w_back, n_expert, n_context):
+    group, halves, slab, width = resid_m.shape
+    seqs = group // n_expert
     n = n_expert * n_context
-    rows = halves * slab
-    resid = resid_low.reshape(group, rows, width).astype(F32)
-    cot = cot.reshape(group, rows, width)
-    here = valid_m.reshape(group, rows) > 0
-    normed, norm_back = jax.vjp(lambda r, g: normalized(r)[0] * g, resid, gain_mix)
-    u = normed.astype(BF)
-    logits = jnp.einsum("spd,de->spe", u, w_control, preferred_element_type=F32)
-    masked = jnp.where(here[..., None], logits, NEG_FILL)
-    weights = jax.nn.softmax(masked, 0)
-    low = weights.astype(BF)
-
-    def to_owner(x):
-        return lax.all_to_all(x, ("expert", "context"), 0, 0)
-
-    mixed = to_owner(jnp.einsum("spe,spd->epd", low, u, preferred_element_type=F32).astype(BF))
-    dexp = to_owner(jnp.einsum("spe,spd->epd", low, cot, preferred_element_type=F32).astype(BF))
-    x = mixed.reshape(n * rows, width)
-    de = dexp.reshape(n * rows, width)
-    pre = dot(x, w_in1)
-    act, gelu_back = jax.vjp(jax.nn.gelu, pre)
-    act = act.astype(BF)
-    eo = dot(act, w_back1).astype(BF)
-    grad_back = dot(act, de, ((0,), (0,)))
-    d_pre = gelu_back(dot(de, w_back1, ((1,), (1,))))[0].astype(BF)
-    grad_in = dot(x, d_pre, ((0,), (0,)))
-    dm = dot(d_pre, w_in1, ((1,), (1,))).astype(BF)
-    eo = to_owner(eo.reshape(n, rows, width))
-    dm = to_owner(dm.reshape(n, rows, width))
-    mix_out = jnp.einsum("spe,epd->spd", low, eo, preferred_element_type=F32)
-    out_full = resid + mix_out
-    d_w = jnp.einsum("spd,epd->spe", cot, eo, preferred_element_type=F32) + jnp.einsum(
-        "spd,epd->spe", u, dm, preferred_element_type=F32
-    )
-    d_logits = (weights * (d_w - jnp.sum(weights * d_w, 0))).astype(BF)
-    grad_control = jnp.einsum("spd,spe->de", u, d_logits, preferred_element_type=F32)
-    d_u = jnp.einsum("spe,de->spd", d_logits, w_control, preferred_element_type=F32) + jnp.einsum(
-        "spe,epd->spd", low, dm, preferred_element_type=F32
-    )
-    d_norm, grad_gain_mix = norm_back(d_u)
-    d_attn = (cot.astype(F32) + d_norm).astype(BF)
-    okf = here.astype(F32)[..., None]
-    sums = jnp.stack([jnp.sum(okf * out_full * out_full), jnp.sum(okf * mix_out * mix_out), jnp.sum(okf)])
-    shape = (group, halves, slab, width)
-    return d_attn.reshape(shape), out_full.astype(BF).reshape(shape), grad_in, grad_back, grad_control, grad_gain_mix, sums
-
-
-def back_phase(d_attn, tok_a, qkv, att, lse, kmark, qmark, gain, wqkv, wout):
+    ff = w_in.shape[-1]
+    span = max(16, 256 // group)
+    steps = slab // span
+    sem = pltpu.SemaphoreType.DMA
+    block = pltpu.VMEM((group, halves, slab, width), BF)
+    turned = pltpu.VMEM((halves, n, slab, width), BF)
+    return pl.pallas_call(
+        functools.partial(mix_kernel, n_expert=n_expert, n_context=n_context),
+        out_shape=(
+            jax.ShapeDtypeStruct((seqs, halves, slab * n_expert, width), BF),
+            jax.ShapeDtypeStruct((group, halves, slab, width), BF),
+            jax.ShapeDtypeStruct((width, ff), BF),
+            jax.ShapeDtypeStruct((width, ff), BF),
+            jax.ShapeDtypeStruct((width, n), F32),
+            jax.ShapeDtypeStruct((1, width), F32),
+            jax.ShapeDtypeStruct((2, width), F32),
+        ),
+        in_specs=[ANY, ANY, VM, VM, VM, ANY, ANY],
+        out_specs=(ANY, ANY, ANY, ANY, VM, VM, VM),
+        scratch_shapes=[
+            block, block, block,
+            pltpu.VMEM((halves * steps, group * span, n), F32),
+            pltpu.VMEM((halves * steps, group * span, n * span), BF),
+            turned, turned, turned, turned, turned, turned, turned, turned,
+            pltpu.VMEM((width, ff), BF), pltpu.VMEM((ff, width), BF),
+            pltpu.VMEM((width, ff), F32), pltpu.VMEM((width, ff), F32),
+            block, block, pltpu.VMEM((2, width, ff), BF),
+            sem((2, halves, n)), sem((2, halves, n)),
+            sem((2, halves, n)), sem((2, halves, n)),
+            sem((halves, n_expert)), sem((halves, n_expert)),
+            sem((4,)), sem((3,)),
+        ],
+        compiler_params=pltpu.CompilerParams(
+            collective_id=1, has_side_effects=True, vmem_limit_bytes=VMEM_LIMIT
+        ),
+        name="mix_and_experts",
+    )(resid_m, cot_m, ok_m, gain, wc, w_in, w_back)
+
+
+def backward_kernel(
+    d_attn, tok_a, qkv_a, att_a, lse, kmark, qmark, gain, wqkv, wout, out_m,
+    dtok_o, out_o, gq_o, go_o, gg_o,
+    da, tok, qkv, att, datt, dkv, dqkv, dtok, bias,
+    out_s, out_r, tok_s, tok_r, in_s, own_s,
+    *, n_expert, n_context,
+):
+    e, c, me, n, peer = ring(n_expert, n_context)
+    seqs, length, width = da.shape
+    half = length // n_context
+    slab = half // n_expert
+    qn = 256
+    loads = [
+        pltpu.make_async_copy(src, dst, in_s.at[i])
+        for i, (src, dst) in enumerate(((d_attn, da), (att_a, att), (qkv_a, qkv), (tok_a, tok)))
+    ]
+    for cp in loads:
+        cp.start()
+    enter(peer, n)
+    crossing = []
+    mine = pl.ds(pl.multiple_of(e * slab, slab), slab)
+    for k in range(1, n):
+        j, pe, pc = peer(k)
+        cp = pltpu.make_async_remote_copy(
+            src_ref=out_m.at[pl.ds(pe * seqs, seqs), pc], dst_ref=out_o.at[c, :, mine, :],
+            send_sem=out_s.at[k], recv_sem=out_r.at[k],
+            device_id={"expert": pe, "context": pc}, device_id_type=MESH,
+        )
+        cp.start()
+        crossing.append(cp)
+    cp = pltpu.make_async_copy(
+        out_m.at[pl.ds(e * seqs, seqs), c], out_o.at[c, :, mine, :], own_s.at[0, 0]
+    )
+    cp.start()
+    crossing.append(cp)
+    lane = lax.broadcasted_iota(jnp.int32, (qn, 128), 1)
+    gg_o[...] = jnp.zeros_like(gg_o)
+    for i in range(4):
+        loads[i].wait()
+    for s in range(seqs):
+        datt[...] = dot(da[s], wout[...], ((1,), (1,))).astype(BF)
+        go = dot(att[s], da[s], ((0,), (0,)))
+        go_o[...] = go if s == 0 else go_o[...] + go
+        dkv[...] = jnp.zeros_like(dkv)
+        for qb in range(length // qn):
+            kk = (qb + 1) * qn
+            rows = pl.ds(qb * qn, qn)
+            mask_bias(bias, kmark, qmark, s, qb * qn, qn)
+
+            def pair(hp, _):
+                at = pl.multiple_of(hp * 128, 128)
+                q2 = qkv[s, rows, pl.ds(at, 128)] * BF(0.125)
+                k2 = qkv[s, pl.ds(0, kk), pl.ds(width + at, 128)]
+                v2 = qkv[s, pl.ds(0, kk), pl.ds(2 * width + at, 128)]
+                do2 = datt[rows, pl.ds(at, 128)]
+                dqs, dss, lows, qms, doms = [], [], [], [], []
+                for h in range(2):
+                    mine = (lane >= 64) if h else (lane < 64)
+                    qm = jnp.where(mine, q2, jnp.zeros_like(q2))
+                    dom = jnp.where(mine, do2, jnp.zeros_like(do2))
+                    st = dot(k2, qm, ((1,), (1,))) + bias[pl.ds(0, kk), :]
+                    p = jnp.exp(st - lse[s, pl.ds(2 * hp + h, 1), rows])
+                    dp = dot(v2, dom, ((1,), (1,)))
+                    delta = jnp.sum(p * dp, 0, keepdims=True)
+                    ds = (p * (dp - delta)).astype(BF)
+                    dqs.append(dot(ds, k2, ((0,), (0,))))
+                    dss.append(ds)
+                    lows.append(p.astype(BF))
+                    qms.append(qm)
+                    doms.append(dom)
+                dqkv[rows, pl.ds(at, 128)] = (jnp.where(lane < 64, dqs[0], dqs[1]) * 0.125).astype(BF)
+                dkv[pl.ds(0, kk), pl.ds(at, 128)] += dot(dss[0], qms[0]) + dot(dss[1], qms[1])
+                dkv[pl.ds(0, kk), pl.ds(width + at, 128)] += dot(lows[0], doms[0]) + dot(
+                    lows[1], doms[1]
+                )
+                return 0
+
+            lax.fori_loop(0, width // 128, pair, 0)
+        dqkv[:, pl.ds(width, 2 * width)] = dkv[...].astype(BF)
+        for h in range(n_context):
+            rows = pl.ds(h * half, half)
+            normed, rstd = normalized(tok[s, h].astype(F32))
+            a = (normed * gain[...]).astype(BF)
+            gq = dot(a, dqkv[rows, :], ((0,), (0,)))
+            gq_o[...] = gq if s == 0 and h == 0 else gq_o[...] + gq
+            d_a = dot(dqkv[rows, :], wqkv[...], ((1,), (1,)))
+            gg_o[...] += jnp.sum(d_a * normed, 0, keepdims=True)
+            q = d_a * gain[...]
+            dt = da[s, rows, :].astype(F32) + rstd * (
+                q - jnp.mean(q, -1, keepdims=True) - normed * jnp.mean(q * normed, -1, keepdims=True)
+            )
+            dtok[s, h] = dt.astype(BF)
+        for k in range(1, n_context):
+            pc = lax.rem(c + k, n_context)
+            cp = pltpu.make_async_remote_copy(
+                src_ref=dtok.at[s, pc], dst_ref=dtok_o.at[c, s],
+                send_sem=tok_s.at[s, k], recv_sem=tok_r.at[s, k],
+                device_id={"context": pc}, device_id_type=MESH,
+            )
+            cp.start()
+            crossing.append(cp)
+        cp = pltpu.make_async_copy(dtok.at[s, c], dtok_o.at[c, s], own_s.at[1, s])
+        cp.start()
+        crossing.append(cp)
+    for cp in crossing:
+        cp.wait()
+
+
+def backward(d_attn, tok_a, qkv, att, lse, kmark, qmark, gain, wqkv, wout, out_m, n_expert, n_context):
     seqs, length, width = d_attn.shape
-    x = tok_a.astype(F32)
-    normed, norm_back = jax.vjp(lambda r, g: normalized(r)[0] * g, x, gain)
-    a = normed.astype(BF)
-    grad_out = jnp.einsum("sld,sle->de", att, d_attn, preferred_element_type=F32)
-    d_att = jnp.einsum("sle,de->sld", d_attn, wout, preferred_element_type=F32).astype(BF)
-
-    def one(pack):
-        qkv, d_att, lse, km, qm = pack
-        q, k, v = (t.reshape(length, HEADS, -1) for t in jnp.split(qkv, 3, -1))
-        do = d_att.reshape(length, HEADS, -1)
-        i = jnp.arange(length)
-        ok = (i[:, None] >= i[None, :]) & (km.T == qm.T)
-        s = jnp.where(ok[None], jnp.einsum("qhd,khd->hqk", q, k, preferred_element_type=F32) * 0.125, NEG_FILL)
-        p = jnp.exp(s - lse[..., None])
-        dp = jnp.einsum("qhd,khd->hqk", do, v, preferred_element_type=F32)
-        ds = (p * (dp - jnp.sum(p * dp, -1, keepdims=True))).astype(BF)
-        dq = jnp.einsum("hqk,khd->qhd", ds, k, preferred_element_type=F32) * 0.125
-        dk = jnp.einsum("hqk,qhd->khd", ds, q, preferred_element_type=F32) * 0.125
-        dv = jnp.einsum("hqk,qhd->khd", p.astype(BF), do, preferred_element_type=F32)
-        return jnp.concatenate([t.reshape(length, width) for t in (dq, dk, dv)], -1).astype(BF)
-
-    d_qkv = lax.map(one, (qkv, d_att, lse, kmark, qmark))
-    grad_qkv = jnp.einsum("sld,slc->dc", a, d_qkv, preferred_element_type=F32)
-    d_a = jnp.einsum("slc,dc->sld", d_qkv, wqkv, preferred_element_type=F32)
-    d_norm, grad_gain = norm_back(d_a)
-    return (d_attn.astype(F32) + d_norm).astype(BF), grad_qkv, grad_out, grad_gain
+    half = length // n_context
+    n = n_expert * n_context
+    sem = pltpu.SemaphoreType.DMA
+    return pl.pallas_call(
+        functools.partial(backward_kernel, n_expert=n_expert, n_context=n_context),
+        out_shape=(
+            jax.ShapeDtypeStruct((n_context, seqs, half, width), BF),
+            jax.ShapeDtypeStruct((n_context, seqs, half, width), BF),
+            jax.ShapeDtypeStruct((width, 3 * width), F32),
+            jax.ShapeDtypeStruct((width, width), F32),
+            jax.ShapeDtypeStruct((1, width), F32),
+        ),
+        in_specs=[ANY, ANY, ANY, ANY, VM, VM, VM, VM, VM, VM, ANY],
+        out_specs=(ANY, ANY, VM, VM, VM),
+        scratch_shapes=[
+            pltpu.VMEM((seqs, length, width), BF),
+            pltpu.VMEM((seqs, n_context, half, width), BF),
+            pltpu.VMEM((seqs, length, 3 * width), BF),
+            pltpu.VMEM((seqs, length, width), BF),
+            pltpu.VMEM((length, width), BF),
+            pltpu.VMEM((length, 2 * width), F32),
+            pltpu.VMEM((length, 3 * width), BF),
+            pltpu.VMEM((seqs, n_context, half, width), BF),
+            pltpu.VMEM((length, 256), F32),
+            sem((n,)), sem((n,)),
+            sem((seqs, n_context)), sem((seqs, n_context)),
+            sem((4,)), sem((2, max(seqs, 1))),
+        ],
+        compiler_params=pltpu.CompilerParams(
+            collective_id=2, has_side_effects=True, vmem_limit_bytes=VMEM_LIMIT
+        ),
+        name="attend_backward",
+    )(d_attn, tok_a, qkv, att, lse, kmark, qmark, gain, wqkv, wout, out_m)
 
 
 def per_device(n_expert, n_context, tokens, gain_attn, wqkv, w_out, gain_mix, w_control, w_in, w_back, segments, valid, cotangent):
@@ -321,36 +625,28 @@
     resid_m, cot_m, tok_a, qkv, att, lse, sq = forward(
         tokens, cotangent, kmark, qmark, gain_attn[None], wqkv, w_out, n_expert, n_context
     )
-    d_attn_m, out_m, grad_in, grad_back, grad_control, grad_gain_mix, sums = mix_phase(
-        resid_m, cot_m, valid_m, gain_mix, w_control, pick(w_in, c), pick(w_back, c), n_expert, n_context
-    )
-    d_attn = lax.all_to_all(d_attn_m, "expert", 0, 2, tiled=True).reshape(seqs, length, width)
-
-    def home(x):
-        x = x.reshape(n_expert, seqs, n_context, slab, width).transpose(0, 2, 1, 3, 4)
-        x = x.reshape(n_expert * n_context, seqs, slab, width)
-        x = lax.all_to_all(x, ("expert", "context"), 0, 0).reshape(n_expert, n_context, seqs, slab, width)
-        return x.transpose(1, 2, 0, 3, 4).reshape(reps, seqs, half, width)
-
-    output = home(out_m)
-    d_tok, grad_qkv, grad_out, grad_gain = back_phase(
-        d_attn, tok_a.reshape(seqs, length, width), qkv, att, lse, kmark, qmark, gain_attn, wqkv, w_out
-    )
-    d_tok = d_tok.reshape(seqs, n_context, half, width).transpose(1, 0, 2, 3)
-    d_tokens = lax.all_to_all(d_tok, "context", 0, 0)
+    d_attn, out_m, grad_in, grad_back_t, grad_control, grad_gain_mix, sq_mix = mix(
+        resid_m, cot_m, valid_m[..., None], gain_mix[None], w_control, w_in, w_back, n_expert, n_context
+    )
+    d_tokens, output, grad_qkv, grad_out, grad_gain = backward(
+        d_attn.reshape(seqs, length, width), tok_a, qkv, att, lse, kmark, qmark, gain_attn[None],
+        wqkv, w_out, out_m, n_expert, n_context,
+    )
 
     def whole(g):
-        g = lax.psum(g.astype(BF), "dp")
-        return lax.all_gather(g, "context").astype(F32)
-
-    squares = jnp.stack([sums[0], jnp.sum(sq), sums[1], sums[2]])
+        return lax.all_gather(lax.psum(g, "dp"), "context").astype(F32)
+
+    squares = jnp.stack(
+        [jnp.sum(sq_mix[0]), jnp.sum(sq), jnp.sum(sq_mix[1]), jnp.sum((valid_m > 0).astype(F32))]
+    )
     grad_gain, grad_qkv, grad_out, grad_gain_mix, grad_control, squares = lax.psum(
-        (grad_gain, grad_qkv, grad_out, grad_gain_mix, grad_control, squares), ("expert", "context", "dp")
+        (grad_gain[0], grad_qkv, grad_out, grad_gain_mix[0], grad_control, squares),
+        ("expert", "context", "dp"),
     )
     stats = jnp.sqrt(squares[:3] / (squares[3] * width))
     return (
         output, d_tokens, grad_gain, grad_qkv, grad_out, grad_gain_mix, grad_control,
-        whole(grad_in), whole(grad_back), stats,
+        whole(grad_in), whole(grad_back_t).transpose(0, 2, 1), stats,
     )
 
 

time: 857 us -> 678 us (0.79)
  matrix products: 270 us -> 0 us
  Pallas kernels: 87.5 us -> 295 us
  other arithmetic: 105 us -> 19 us
  waiting for transfers between devices: 214 us -> 268 us
  local copies, waits for them, and re-layouts: 59.9 us -> 23.2 us
  starting transfers between devices: 32.7 us -> 0.16 us
  blocking collectives: 63.9 us -> 52.8 us
    dot_general x29 -> x0, matrix products: 270 us -> none  [the longest x6 68.7 us: dot(): return lax.dot_general(a, b, (dims, ((), ())), preferred_element_type=F32)]
    pallas_call x0 -> x2, Pallas kernels: none -> 207 us  [the longest x1 123 us: mix(): pl.pallas_call(functools.partial(mix_kernel, n_expert=n_expert, n_context...]
    all_gather x2, waiting for transfers between devices: 0.01 us -> 99.8 us  [whole(): return lax.all_gather(lax.psum(g, 'dp'), 'context').astype(F32)]
    convert_element_type x11 -> x1, other arithmetic: 78.4 us -> 6.65 us  [whole(): return lax.all_gather(lax.psum(g, 'dp'), 'context').astype(F32)]
    all_to_all x7 -> x0, waiting for transfers between devices: 65.6 us -> none  [the longest x4 56.3 us: to_owner(): return lax.all_to_all(x, ('expert', 'context'), 0, 0)]
    all_to_all x7 -> x0, starting transfers between devices: 32.3 us -> none  [the longest x4 17.9 us: to_owner(): return lax.all_to_all(x, ('expert', 'context'), 0, 0)]
    dynamic_slice x12 -> x0, local copies, waits for them, and re-layouts: 22 us -> none  [back_phase(): d_qkv = lax.map(one, (qkv, d_att, lse, kmark, qmark))]
    psum x2, waiting for transfers between devices: 149 us -> 168 us  [the longest x1 95.3 us: per_device(): lax.psum((grad_gain[0], grad_qkv, grad_out, grad_gain_mix[0], grad_contro...]
  transfers between devices with their start and end apart: 11 -> 4, of which waited for: 7 -> 4; matrix products, arithmetic and copies ran while one was open for 44% -> 3% of each run, Pallas kernels for 0% -> 13%
where the time goes in v2:
time: 678 us; the launch traced here: 673 us
  Pallas kernels  295 us (44%)
  waiting for transfers between devices  268 us (40%)
  blocking collectives  52.8 us (8%)
  local copies, waits for them, and re-layouts  23.2 us (3%)
  other arithmetic  19 us (3%)
  between operations  14.8 us (2%)
    pallas_call x1, Pallas kernels, mix(): pl.pallas_call(functools.partial(mix_kernel, n_expert=n_expert, n_context...  123 us
    all_gather x2, waiting for transfers between devices, whole(): return lax.all_gather(lax.psum(g, 'dp'), 'context').astype(F32)  99.8 us
    psum x1, waiting for transfers between devices, per_device(): lax.psum((grad_gain[0], grad_qkv, grad_out, grad_gain_mix[0], grad_contro...  95.3 us
    pallas_call x1, Pallas kernels, forward(): pl.pallas_call(functools.partial(forward_kernel, n_expert=n_expert, n_con...  87.4 us
    pallas_call x1, Pallas kernels, backward(): pl.pallas_call(functools.partial(backward_kernel, n_expert=n_expert, n_co...  84.2 us
    psum x1, waiting for transfers between devices, whole(): return lax.all_gather(lax.psum(g, 'dp'), 'context').astype(F32)  72.7 us
    psum x1, blocking collectives, per_device(): lax.psum((grad_gain[0], grad_qkv, grad_out, grad_gain_mix[0], grad_contro...  46.4 us
    unnamed x26, local copies, waits for them, and re-layouts  19.3 us
  transfers between devices with their start and end apart: 4, of which 4 were waited for; matrix products, arithmetic and copies ran while one was open for 3% of the time, Pallas kernels for 13%

profile of v2, /device:TPU:0, one launch (start us, length us, event | category | flops | bytes accessed | tf_op | source)
XLA Modules:
  0.0 673.3 jit_solution(14525128793949678554)
XLA Ops:
  7.2 0.0 all-reduce.8.cloned.1.call-start
  7.2 6.5 all-gather
  13.7 0.7 constant_dynamic-slice_fusion.1
  14.4 0.6 broadcast_in_dim.19.qmark
  15.1 1.5 copy.36.wc
  16.5 0.6 fusion.1
  17.2 1.3 copy.35.ok_m
  18.5 1.3 copy.32.kmark
  19.9 87.4 %attend_forward.1 = (bf16[8,2,128,512]{3,2,1,0:T(8,128)(2,1)}, bf16[8,2,128,512]{3,2,1,0:T(8,128)(2,1)}, bf16[2,2,512,512]{3,2,1,0:T(8,128)(2,1)}, bf16[2,1024,1...) custom-call(bf16[2,2,512,512]{3,2,1,0:T(8,128)(2,1)} %tokens.1, ...), custom_call_target="tpu_custom_call" | custom-call | tf_op jit(solution)/shard_map/attend_forward/pallas_call | solution.py:196
  107.3 123.3 %mix_and_experts.1 = (bf16[2,2,512,512]{3,2,1,0:T(8,128)(2,1)}, bf16[8,2,128,512]{3,2,1,0:T(8,128)(2,1)}, bf16[512,2048]{1,0:T(8,128)(2,1)}, bf16[512,2048]{1,0:...) custom-call(bf16[8,2,128,512]{3,2,1,0:T(8,128)(2,1)} %get-tuple-element.29.resid_m, ...), custom_call_target="tpu_custom_call" | custom-call | tf_op jit(solution)/shard_map/mix_and_experts/pallas_call | solution.py:432
  230.6 0.0 all-reduce.8.cloned.1.call-update
  230.6 0.0 all-reduce.6.cloned.1.call-start
  230.6 84.2 %attend_backward.1 = (bf16[2,2,512,512]{3,2,1,0:T(8,128)(2,1)}, bf16[2,2,512,512]{3,2,1,0:T(8,128)(2,1)}, f32[512,1536]{1,0:T(8,128)}, f32[512,512]{1,0:T(8,128)}, f32[1,512]{1,0:T(1,128)}) custom-call(bf16[2,1024,512]{2,1,0:T(8,128)(2,1)} %bitcast.22, bf16[2,2,512,512]{3,2,1,0:T(8,128)(2,1)} %get-tuple-element.32.tok_a, ...), custom_call_target="tpu_custom_call" | custom-call | tf_op jit(solution)/shard_map/attend_backward/pallas_call | solution.py:578
  314.9 0.0 all-reduce.6.cloned.1.call-update
  314.9 0.0 all-gather.6.cloned.1.call-start
  315.0 72.7 %all-reduce.8.cloned.1.call-done = (bf16[1,512,2048]{2,1,0:T(8,128)(2,1)}, bf16[1,512,2048]{2,1,0:T(8,128)(2,1)}) async-done(((bf16[1,512,2048]{2,1,0:T(8,128)(2,1)}, bf16[1,512,2048]{2,1,0:T(8,128)(2,1)}), (bf16[1,512,2048]{2,1,0:T(8,128)(2,1)}, bf16[1,512,2048]{2,1,0:T(8,128)(2,1)})) %all-reduce.8.cloned.1.call-update) | async-done | bytes 4194320 | tf_op jit(solution)/shard_map/psum | solution.py:637
  387.7 0.0 copy-start.8
  387.7 0.0 copy-start.5
  387.7 0.0 copy-start.4
  387.7 0.0 all-gather.6.cloned.1.call-update
  387.7 0.0 all-gather.4.cloned.1.call-start
  387.7 0.5 all-gather.4.cloned.1.call-update
  388.3 0.1 copy-done.8
  388.3 0.6 reduce_sum.37
  388.9 0.0 copy-done.5
  388.9 0.6 slice_reduce_fusion.1
  389.5 2.7 pad_maximum_fusion
  392.2 0.0 copy-done.4
  392.2 0.0 copy-done.6
  392.2 0.0 copy-done.7
  392.2 46.4 %all-reduce = (f32[512]{0:T(512)}, f32[512]{0:T(512)}, f32[512,8]{1,0:T(8,128)S(1)}, f32[4]{0:T(128)S(1)}) all-reduce(f32[512]{0:T(512)S(1)} %bitcast.31, f32[512]{0:T(512)S(1)} %bitcast.30, f32[512,8]{1,0:T(8,128)S(1)} %copy-done.4, f32[4]{0:T(128)S(1)} %pad_maximum_fusion), channel_id=1, replica_groups=mesh['expert'=4,'context'=2,'dp'=4] {'expert','context','dp'}, use_global_device_ids=true, to_apply=%region_0.1 | all-reduce | flops 5124 | bytes 40992 | tf_op jit(solution)/shard_map/psum | solution.py:642
  438.6 0.6 slice.15
  439.2 0.7 copy.38
  440.5 0.5 divide_sqrt_fusion
  441.0 95.3 %all-reduce.6.cloned.1.call-done = (f32[512,1536]{1,0:T(8,128)}, f32[512,512]{1,0:T(8,128)}) async-done(((f32[512,1536]{1,0:T(8,128)}, f32[512,512]{1,0:T(8,128)}), (f32[512,1536]{1,0:T(8,128)}, f32[512,512]{1,0:T(8,128)})) %all-reduce.6.cloned.1.call-update) | async-done | bytes 4194320 | tf_op jit(solution)/shard_map/psum | solution.py:642
  536.4 57.3 %all-gather.6.cloned.1.call-done = bf16[2,512,2048]{2,1,0:T(8,128)(2,1)} async-done(((bf16[1,512,2048]{2,1,0:T(8,128)(2,1)}), bf16[2,512,2048]{2,1,0:T(8,128)(2,1)}) %all-gather.6.cloned.1.call-update) | async-done | bytes 4194320 | tf_op jit(solution)/shard_map/all_gather | solution.py:637
  593.7 6.7 convert_bitcast_fusion
  600.3 9.1 %copy.39 = f32[2,2048,512]{2,1,0:T(8,128)} copy(f32[2,2048,512]{1,2,0:T(8,128)} %convert_bitcast_fusion) | data formatting | bytes 16777216
  609.4 42.5 %all-gather.4.cloned.1.call-done = bf16[2,512,2048]{2,1,0:T(8,128)(2,1)} async-done(((bf16[1,512,2048]{2,1,0:T(8,128)(2,1)}), bf16[2,512,2048]{2,1,0:T(8,128)(2,1)}) %all-gather.4.cloned.1.call-update) | async-done | bytes 4194320 | tf_op jit(solution)/shard_map/all_gather | solution.py:637
  651.9 6.7 convert_element_type.8
  658.6 0.0 copy-done.2
  658.6 1.3 copy.51
  659.9 1.0 copy-done.1
  660.9 1.3 copy.52
  662.3 1.3 copy-done
  663.6 1.7 copy.53
  665.3 0.3 copy-done.3
  665.5 1.0 copy.54
  (8 shorter events, 0.0 us)
Async XLA Ops:
  7.2 380.5 %all-reduce.8.cloned.1.call-start = ((), (), s32[]{:S(2)}) async-start(), calls=%async_computation.3 | async-start | bytes 8388608 | tf_op jit(solution)/shard_map/psum | solution.py:637
  230.6 305.8 %all-reduce.6.cloned.1.call-start = ((), (), s32[]{:S(2)}) async-start(), calls=%async_computation.2 | async-start | bytes 8388608 | tf_op jit(solution)/shard_map/psum | solution.py:642
  314.9 278.8 %all-gather.6.cloned.1.call-start = ((), (), s32[]{:S(2)}) async-start(), calls=%async_computation.1 | async-start | bytes 6291456 | tf_op jit(solution)/shard_map/all_gather | solution.py:637
  387.7 0.7 copy-start.8
  387.7 1.3 copy-start.5
  387.7 4.5 copy-start.4
  387.7 4.5 copy-start.6
  387.7 4.5 copy-start.7
  387.7 264.2 %all-gather.4.cloned.1.call-start = ((), (), s32[]{:S(2)}) async-start(), calls=%async_computation | async-start | bytes 6291456 | tf_op jit(solution)/shard_map/all_gather | solution.py:637
  609.4 49.1 %copy-start.2 = (bf16[2,2,512,512]{3,2,1,0:T(8,128)(2,1)S(1)}, bf16[2,2,512,512]{3,2,1,0:T(8,128)(2,1)}, u32[]{:S(2)}) copy-start(bf16[2,2,512,512]{3,2,1,0:T(8,128)(2,1)} %get-tuple-element.102) | copy-start | bytes 6291460
  658.6 2.3 copy-start.1
  660.9 2.6 copy-start
  663.6 2.0 copy-start.3
Sparse Core Ops, SparseCore 0:
  230.7 156.9 all-reduce.7
  394.3 142.0 all-reduce.5
  538.0 55.6 all-gather.5
  595.2 56.7 all-gather.3
